TPU v7x, 256 devices: a whole 4x4x8 slice. The times are simulated.
256 devices in a mesh: lat: 4 (over y_hi, core), lon: 64 (over z, y_lo, x).
Axes of the slice: x: 4, y: 4 (y_hi: 2, y_lo: 2; y = y_hi * 2 + y_lo), z: 8, core: 2. Of those that a mesh axis runs over, the one named last changes fastest.
Arguments:
- grid_latent: bfloat16 [4, 64, 128, 512], P('lat', 'lon'), may hold values from -16 to 16
- grid_cot: bfloat16 [4, 64, 128, 512], P('lat', 'lon'), may hold values from -6 to 6
- mesh_latent: bfloat16 [4, 64, 64, 512], P('lat', 'lon'), may hold values from -16 to 16
- mesh_cot: bfloat16 [4, 64, 64, 512], P('lat', 'lon'), may hold values from -6 to 6
- processed: bfloat16 [4, 64, 64, 512], P('lat', 'lon'), may hold values from -16 to 16
- enc_weights: bfloat16 [3, 512, 512], replicated, may hold values from -0.25 to 0.25
- dec_weights: bfloat16 [3, 512, 512], replicated, may hold values from -0.25 to 0.25
- enc_send: int32 [4, 64, 2, 128], P('lat', 'lon'), may hold values from 0 to 127
- enc_recv: int32 [4, 64, 2, 128], P('lat', 'lon'), may hold values from 0 to 575, as said below
- enc_live: int32 [4, 64, 1], P('lat', 'lon'), may hold values from 64 to 256
- dec_send: int32 [4, 64, 3, 128], P('lat', 'lon'), may hold values from 0 to 575, as said below
- dec_recv: int32 [4, 64, 3, 128], P('lat', 'lon'), may hold values from 0 to 127
Outputs:
- grid_grad: bfloat16 [4, 64, 128, 512], P('lat', 'lon')
- mesh_grad: bfloat16 [4, 64, 64, 512], P('lat', 'lon')
- proc_grad: bfloat16 [4, 64, 64, 512], P('lat', 'lon')
- enc_grads: float32 [3, 512, 512], P(None, 'lon')
- dec_grads: float32 [3, 512, 512], P(None, 'lon')
Inputs may be any that keep to these rules, and one draw needn't show every extreme that they name: `enc_recv`: row e names slot e // 64 = 3 a + b of the extended block (band offset a - 1, sector offset b - 1, sectors closed in a cycle); no edge names a band outside the grid. `dec_send`: row e names slot e // 64 = 3 a + b of the extended block (band offset a - 1, sector offset b - 1, sectors closed in a cycle); no edge names a band outside the grid. The first enc_live[t] slots of tile t are live.
All inputs are finite; a program needn't handle non-finite values.
Results may differ from a plain program's by a relative error of at most 0.006.
Values may be sent and summed in bfloat16 or wider, within the bound.
A program may use at most 128 MiB of HBM per device.

v0:
```python
import math

import jax
import jax.numpy as jnp
from jax import lax
from jax.sharding import PartitionSpec as P


def padded(block, sides, width, periodic):
    for axis, dim in sides:
        count = lax.axis_size(axis)
        forward = [(i, i + 1) for i in range(count - 1)]
        if periodic:
            forward.append((count - 1, 0))
        backward = [(target, source) for source, target in forward]
        low = lax.ppermute(
            lax.slice_in_dim(block, block.shape[dim] - width, None, axis=dim), axis, forward
        )
        high = lax.ppermute(lax.slice_in_dim(block, 0, width, axis=dim), axis, backward)
        block = jnp.concatenate([low, block, high], axis=dim)
    return block


def shifted(block, axis, distance):
    devices = range(lax.axis_size(axis))
    route = [((i - distance) % len(devices), i) for i in devices]
    return lax.ppermute(block, axis, route)


def passed_along(value, axis, steps):
    count = lax.axis_size(axis)
    leading, last = (max(0, -steps), min(count, count - steps))
    return lax.ppermute(value, axis, [(source, source + steps) for source in range(leading, last)])


def silu_slope(values):
    gate_sig = jax.nn.sigmoid(values)
    return gate_sig * (1.0 + values * (1.0 - gate_sig))


def project(row_block, weight):
    return jnp.dot(row_block, weight, preferred_element_type=jnp.float32)


def project_back(row_block, weight):
    return lax.dot_general(
        row_block, weight, (((1,), (1,)), ((), ())), preferred_element_type=jnp.float32
    )


def transpose_product(left_rows, right_rows):
    return lax.dot_general(
        left_rows, right_rows, (((0,), (0,)), ((), ())), preferred_element_type=jnp.float32
    )


def one_hot(indices, columns):
    return (indices[:, None] == lax.broadcasted_iota(jnp.int32, (1, columns), 1)).astype(
        jnp.bfloat16
    )


def rim_lon(mesh_field):
    return padded(mesh_field, (("lon", 1),), 1, True)


def rim_lat(mesh_field):
    return padded(mesh_field, (("lat", 0),), 1, False)


def fold_lon(low_slot, middle, high_slot):
    return middle + shifted(high_slot, "lon", 1) + shifted(low_slot, "lon", -1)


def fold_lat(low_slot, middle, high_slot):
    return middle + passed_along(high_slot, "lat", 1) + passed_along(low_slot, "lat", -1)


def edge_backward(pre_act, cot_picked, live_count, out_weight):
    slot_index = lax.broadcasted_iota(jnp.int32, (pre_act.shape[0], 1), 0)
    hidden = jax.nn.silu(pre_act).astype(jnp.bfloat16)
    msg_grad = jnp.where(slot_index < live_count, cot_picked, 0.0).astype(jnp.bfloat16)
    pre_grad = (project_back(msg_grad, out_weight) * silu_slope(pre_act)).astype(jnp.bfloat16)
    return (pre_grad, transpose_product(hidden, msg_grad))


def shards(
    grid_latent,
    grid_cot,
    mesh_latent,
    mesh_cot,
    processed,
    enc_weights,
    dec_weights,
    enc_send,
    enc_recv,
    enc_live,
    dec_send,
    dec_recv,
):
    grid_rows = grid_latent[0, 0]
    cot_rows = grid_cot[0, 0]
    features = grid_rows.shape[1]
    mesh_rows = mesh_latent.shape[2]
    tile_count = enc_live.shape[2]
    tile_rows = grid_rows.shape[0] // tile_count
    ext_rows = 9 * mesh_rows
    grid_enc = project(grid_rows, enc_weights[0]).astype(jnp.bfloat16)
    grid_dec = project(grid_rows, dec_weights[1]).astype(jnp.bfloat16)
    mesh_enc = project(mesh_latent[0, 0], enc_weights[1]).astype(jnp.bfloat16)
    proc_dec = project(processed[0, 0], dec_weights[0]).astype(jnp.bfloat16)
    stacked = jnp.concatenate([mesh_enc, mesh_cot[0, 0], proc_dec], 0)[None, None]
    extended = rim_lat(rim_lon(stacked))
    extended = extended.reshape(9, 3, mesh_rows, features)
    mesh_ext = extended[:, 0].reshape(ext_rows, features)
    cot_ext = extended[:, 1].reshape(ext_rows, features)
    proc_ext = extended[:, 2].reshape(ext_rows, features)

    def enc_step(state_in, inputs):
        out_grad, mesh_part = state_in
        tile_proj, senders, receivers, live_count = inputs
        grid_pick = one_hot(senders, tile_rows)
        pre_act = project(grid_pick, tile_proj) + jnp.take(mesh_ext, receivers, axis=0).astype(
            jnp.float32
        )
        pre_grad, out_term = edge_backward(
            pre_act, jnp.take(cot_ext, receivers, axis=0), live_count, enc_weights[2]
        )
        grid_sum = transpose_product(grid_pick, pre_grad).astype(jnp.bfloat16)
        mesh_add = jax.ops.segment_sum(
            pre_grad.astype(jnp.float32), receivers, num_segments=ext_rows
        )
        return ((out_grad + out_term, mesh_part + mesh_add), grid_sum)

    def dec_step(state_in, inputs):
        out_grad, mesh_part = state_in
        tile_proj, tile_cot, senders, receivers = inputs
        grid_pick = one_hot(receivers, tile_rows)
        pre_act = jnp.take(proc_ext, senders, axis=0).astype(jnp.float32) + project(
            grid_pick, tile_proj
        )
        pre_grad, out_term = edge_backward(
            pre_act, project(grid_pick, tile_cot), senders.shape[0], dec_weights[2]
        )
        grid_sum = transpose_product(grid_pick, pre_grad).astype(jnp.bfloat16)
        mesh_add = jax.ops.segment_sum(pre_grad.astype(jnp.float32), senders, num_segments=ext_rows)
        return ((out_grad + out_term, mesh_part + mesh_add), grid_sum)

    start = (
        jnp.zeros((features, features), jnp.float32),
        jnp.zeros((ext_rows, features), jnp.float32),
    )
    enc_inputs = (
        grid_enc.reshape(tile_count, tile_rows, features),
        enc_send.reshape(tile_count, -1),
        enc_recv.reshape(tile_count, -1),
        enc_live.reshape(tile_count),
    )
    (enc_out_grad, enc_mesh_part), enc_grid_sum = lax.scan(enc_step, start, enc_inputs)
    dec_inputs = (
        grid_dec.reshape(tile_count, tile_rows, features),
        cot_rows.reshape(tile_count, tile_rows, features),
        dec_send.reshape(tile_count, -1),
        dec_recv.reshape(tile_count, -1),
    )
    (dec_out_grad, dec_mesh_part), dec_grid_sum = lax.scan(dec_step, start, dec_inputs)
    enc_grid_sum = enc_grid_sum.reshape(-1, features)
    dec_grid_sum = dec_grid_sum.reshape(-1, features)
    ghost_sums = jnp.concatenate(
        [
            enc_mesh_part.reshape(3, 3, mesh_rows, features),
            dec_mesh_part.reshape(3, 3, mesh_rows, features),
        ],
        2,
    )
    halfway = fold_lon(ghost_sums[:, 0], ghost_sums[:, 1], ghost_sums[:, 2])
    folded = fold_lat(halfway[0], halfway[1], halfway[2])
    enc_mesh_sum = folded[:mesh_rows].astype(jnp.bfloat16)
    dec_mesh_sum = folded[mesh_rows:].astype(jnp.bfloat16)
    grid_grad = (
        cot_rows.astype(jnp.float32)
        + project_back(enc_grid_sum, enc_weights[0])
        + project_back(dec_grid_sum, dec_weights[1])
    ).astype(jnp.bfloat16)
    mesh_grad = (
        mesh_cot[0, 0].astype(jnp.float32) + project_back(enc_mesh_sum, enc_weights[1])
    ).astype(jnp.bfloat16)
    proc_grad = project_back(dec_mesh_sum, dec_weights[0]).astype(jnp.bfloat16)
    weight_terms = jnp.stack(
        [
            transpose_product(grid_rows, enc_grid_sum),
            transpose_product(mesh_latent[0, 0], enc_mesh_sum),
            enc_out_grad,
            transpose_product(processed[0, 0], dec_mesh_sum),
            transpose_product(grid_rows, dec_grid_sum),
            dec_out_grad,
        ]
    )
    summed = lax.psum(weight_terms, ("lat", "lon"))
    own_rows = features // lax.axis_size("lon")
    summed = lax.dynamic_slice_in_dim(summed, lax.axis_index("lon") * own_rows, own_rows, 1)
    grad_scale = 1.0 / math.sqrt(lax.axis_size("lat") * lax.axis_size("lon") * grid_rows.shape[0])
    enc_grads = summed[:3] * grad_scale
    dec_grads = summed[3:] * grad_scale
    return (
        grid_grad[None, None],
        mesh_grad[None, None],
        proc_grad[None, None],
        enc_grads,
        dec_grads,
    )


def solution(mesh):
    placed = (
        P("lat", "lon", None, None),
        P("lat", "lon", None, None),
        P("lat", "lon", None, None),
        P("lat", "lon", None, None),
        P("lat", "lon", None, None),
        P(),
        P(),
        P("lat", "lon", None, None),
        P("lat", "lon", None, None),
        P("lat", "lon", None),
        P("lat", "lon", None, None),
        P("lat", "lon", None, None),
    )
    return jax.shard_map(
        shards,
        mesh=mesh,
        in_specs=placed,
        out_specs=(
            P("lat", "lon", None, None),
            P("lat", "lon", None, None),
            P("lat", "lon", None, None),
            P(None, "lon", None),
            P(None, "lon", None),
        ),
        check_vma=False,
    )
```

profile of v0, /device:TPU:25, one launch (start us, length us, event | category | flops | bytes accessed | tf_op | source)
XLA Modules:
  0.0 374.8 jit_solution(14015108191969973606)
XLA Ops:
  7.3 1.3 convolution_convert_fusion.5
  8.6 1.3 convolution_convert_fusion.6
  9.9 0.9 maximum_bitcast_fusion
  10.8 2.7 collective-permute-start.1
  14.2 2.9 collective-permute-done.1
  17.1 4.0 %collective-permute-done = bf16[1,1,192,512]{3,2,1,0:T(8,128)(2,1)S(1)} collective-permute-done((bf16[1,1,192,512]{3,2,1,0:T(8,128)(2,1)S(1)}, bf16[1,1,192,512]{3,2,1,0:T(8,128)(2,1)S(1)}, u32[]{:S(2)}, u32[]{:S(2)}) %collective-permute-start) | collective-permute-done | bytes 196640 | tf_op jit(solution)/shard_map/ppermute | solution.py:16
  21.1 0.1 pad_maximum_fusion.2
  21.1 3.8 %collective-permute-start.3 = (bf16[1,3,192,512]{3,2,1,0:T(8,128)(2,1)S(1)}, bf16[1,3,192,512]{3,2,1,0:T(8,128)(2,1)S(1)}, u32[]{:S(2)}, u32[]{:S(2)}) collective-permute-start(bf16[1,3,192,512]{3,2,1,0:T(8,128)(2,1)S(1)} %pad_maximum_fusion.2), channel_id=1, source_target_pairs={{64,0},{128,64},{192,128},{65,1},{129,65},{193,129},{66,2},{130,66... | collective-permute-start | bytes 1769480 | tf_op jit(solution)/shard_map/ppermute | solution.py:19
  24.9 1.3 collective-permute-start.2
  26.3 1.1 fusion.7
  27.4 1.4 collective-permute-done.2
  28.8 0.2 pad_maximum_fusion
  29.1 0.2 fusion.79
  29.2 1.2 gather_fusion.2
  30.4 1.2 gather_fusion.1
  31.6 2.1 gather_fusion
  33.7 1.4 convolution_add_fusion
  35.0 1.8 fusion.6
  36.8 1.5 convolution_add_fusion.1
  38.3 1.6 fusion.8
  40.0 2.4 scatter_custom_fusion
  42.4 3.2 scatter_custom_fusion.1
  45.6 0.2 fusion.15
  45.7 0.1 collective-permute-start.5
  45.8 1.5 collective-permute-start.4
  47.3 0.3 convolution_convert_fusion
  47.6 9.0 %collective-permute-done.5 = f32[3,128,512]{2,1,0:T(8,128)S(1)} collective-permute-done((f32[3,128,512]{2,1,0:T(8,128)S(1)}, f32[3,128,512]{2,1,0:T(8,128)S(1)}, u32[]{:S(2)}, u32[]{:S(2)}) %collective-permute-start.5) | collective-permute-done | bytes 786464 | tf_op jit(solution)/shard_map/ppermute | solution.py:27
  56.6 2.4 collective-permute-done.4
  59.0 0.3 fusion.19
  59.4 12.0 %collective-permute-start.7 = (f32[128,512]{1,0:T(8,128)S(1)}, f32[128,512]{1,0:T(8,128)S(1)}, u32[]{:S(2)}, u32[]{:S(2)}) collective-permute-start(f32[128,512]{1,0:T(8,128)S(1)} %get-tuple-element.72), channel_id=1, source_target_pairs={{64,0},{128,64},{192,128},{65,1},{129,65},{193,129},{66,2},{130,66... | collective-permute-start | bytes 786440 | tf_op jit(solution)/shard_map/ppermute | solution.py:33
  71.4 1.3 collective-permute-start.6
  72.7 0.3 convolution_convert_fusion.3
  73.0 1.3 fusion.5
  74.3 0.5 collective-permute-done.6
  74.9 1.4 fusion.4
  76.2 1.6 fusion
  77.9 1.3 fusion.3
  79.2 1.3 fusion.2
  80.5 1.6 fusion.1
  82.1 1.4 copy-done.3
  83.4 1.2 convolution_add_fusion.3
  84.7 1.0 fusion.10
  85.7 0.9 fusion.13
  86.6 0.9 fusion.12
  87.5 276.8 %all-reduce.2.cloned.1.call-done = f32[6,512,512]{1,2,0:T(8,128)} async-done(((f32[6,512,512]{1,2,0:T(8,128)}), f32[6,512,512]{1,2,0:T(8,128)}) %all-reduce.2.cloned.1.call-update) | async-done | bytes 6291472 | tf_op jit(solution)/shard_map/psum | solution.py:199
  364.3 1.9 dynamic-slice_multiply_fusion
  366.2 0.9 copy.21
  367.1 0.9 copy.22
  (54 shorter events, 0.3 us)
Async XLA Ops:
  7.2 26.5 %copy-start = (bf16[1,1,128,512]{3,2,1,0:T(8,128)(2,1)S(1)}, bf16[1,1,128,512]{3,2,1,0:T(8,128)(2,1)}, u32[]{:S(2)}) copy-start(bf16[1,1,128,512]{3,2,1,0:T(8,128)(2,1)} %param.14) | copy-start | bytes 393220
  7.2 6.3 %copy-start.15 = (s32[1,1,3,128]{3,1,2,0:T(1,128)S(1)}, s32[1,1,3,128]{3,1,2,0:T(1,128)}, u32[]{:S(2)}) copy-start(s32[1,1,3,128]{3,1,2,0:T(1,128)} %param.24) | copy-start | bytes 4612
  7.2 6.3 %copy-start.17 = (s32[1,1,2,128]{3,2,1,0:T(2,128)S(1)}, s32[1,1,2,128]{3,2,1,0:T(2,128)}, u32[]{:S(2)}) copy-start(s32[1,1,2,128]{3,2,1,0:T(2,128)} %param.22) | copy-start | bytes 3076
  7.2 19.1 %copy-start.18 = (s32[1,1,3,128]{3,1,2,0:T(1,128)S(1)}, s32[1,1,3,128]{3,1,2,0:T(1,128)}, u32[]{:S(2)}) copy-start(s32[1,1,3,128]{3,1,2,0:T(1,128)} %param.25) | copy-start | bytes 4612
  7.2 19.1 %copy-start.13 = (bf16[1,1,128,512]{3,2,1,0:T(8,128)(2,1)S(1)}, bf16[1,1,128,512]{3,2,1,0:T(8,128)(2,1)}, u32[]{:S(2)}) copy-start(bf16[1,1,128,512]{3,2,1,0:T(8,128)(2,1)} %param.15) | copy-start | bytes 393220
  7.2 357.1 %all-reduce.2.cloned.1.call-start = ((), (), s32[]{:S(2)}) async-start(), calls=%async_computation | async-start | bytes 12582912 | tf_op jit(solution)/shard_map/psum | solution.py:199
  10.8 6.3 %collective-permute-start.1 = (bf16[1,1,192,512]{3,2,1,0:T(8,128)(2,1)S(1)}, bf16[1,1,192,512]{3,2,1,0:T(8,128)(2,1)S(1)}, u32[]{:S(2)}, u32[]{:S(2)}) collective-permute-start(bf16[1,1,192,512]{3,2,1,0:T(8,128)(2,1)S(1)} %maximum_bitcast_fusion), channel_id=1, source_target_pairs={{1,0},{2,1},{3,2},{4,3},{5,4},{6,5},{7,6},{8,7},{9,8},{10,9},{11,1... | collective-permute-start | bytes 589832 | tf_op jit(solution)/shard_map/ppermute | solution.py:19
  13.5 7.6 %collective-permute-start = (bf16[1,1,192,512]{3,2,1,0:T(8,128)(2,1)S(1)}, bf16[1,1,192,512]{3,2,1,0:T(8,128)(2,1)S(1)}, u32[]{:S(2)}, u32[]{:S(2)}) collective-permute-start(bf16[1,1,192,512]{3,2,1,0:T(8,128)(2,1)S(1)} %maximum_bitcast_fusion), channel_id=1, source_target_pairs={{0,1},{1,2},{2,3},{3,4},{4,5},{5,6},{6,7},{7,8},{8,9},{9,10},{10,1... | collective-permute-start | bytes 589832 | tf_op jit(solution)/shard_map/ppermute | solution.py:16
  21.1 6.3 %collective-permute-start.3 = (bf16[1,3,192,512]{3,2,1,0:T(8,128)(2,1)S(1)}, bf16[1,3,192,512]{3,2,1,0:T(8,128)(2,1)S(1)}, u32[]{:S(2)}, u32[]{:S(2)}) collective-permute-start(bf16[1,3,192,512]{3,2,1,0:T(8,128)(2,1)S(1)} %pad_maximum_fusion.2), channel_id=1, source_target_pairs={{64,0},{128,64},{192,128},{65,1},{129,65},{193,129},{66,2},{130,66... | collective-permute-start | bytes 1769480 | tf_op jit(solution)/shard_map/ppermute | solution.py:19
  24.9 3.9 %collective-permute-start.2 = (bf16[1,3,192,512]{3,2,1,0:T(8,128)(2,1)S(1)}, bf16[1,3,192,512]{3,2,1,0:T(8,128)(2,1)S(1)}, u32[]{:S(2)}, u32[]{:S(2)}) collective-permute-start(bf16[1,3,192,512]{3,2,1,0:T(8,128)(2,1)S(1)} %pad_maximum_fusion.2), channel_id=1, source_target_pairs={{0,64},{64,128},{128,192},{1,65},{65,129},{129,193},{2,66},{66,130... | collective-permute-start | bytes 1769480 | tf_op jit(solution)/shard_map/ppermute | solution.py:16
  31.5 6.8 %copy-start.9 = (bf16[256,512]{1,0:T(8,128)(2,1)}, bf16[256,512]{1,0:T(8,128)(2,1)S(1)}, u32[]{:S(2)}) copy-start(bf16[256,512]{1,0:T(8,128)(2,1)S(1)} %gather_fusion.1) | copy-start | bytes 786436
  31.6 2.1 copy-start.1
  35.0 1.8 copy-start.16
  38.3 1.7 copy-start.5
  45.7 10.9 %collective-permute-start.5 = (f32[3,128,512]{2,1,0:T(8,128)S(1)}, f32[3,128,512]{2,1,0:T(8,128)S(1)}, u32[]{:S(2)}, u32[]{:S(2)}) collective-permute-start(f32[3,128,512]{2,1,0:T(8,128)S(1)} %get-tuple-element.67), channel_id=1, source_target_pairs={{1,0},{2,1},{3,2},{4,3},{5,4},{6,5},{7,6},{8,7},{9,8},{10,9},{11,1... | collective-permute-start | bytes 2359304 | tf_op jit(solution)/shard_map/ppermute | solution.py:27
  45.8 13.2 %collective-permute-start.4 = (f32[3,128,512]{2,1,0:T(8,128)S(1)}, f32[3,128,512]{2,1,0:T(8,128)S(1)}, u32[]{:S(2)}, u32[]{:S(2)}) collective-permute-start(f32[3,128,512]{2,1,0:T(8,128)S(1)} %get-tuple-element.66), channel_id=1, source_target_pairs={{63,0},{0,1},{1,2},{2,3},{3,4},{4,5},{5,6},{6,7},{7,8},{8,9},{9,10... | collective-permute-start | bytes 2359304 | tf_op jit(solution)/shard_map/ppermute | solution.py:27
  59.3 15.5 %copy-start.11 = (bf16[1,1,64,512]{3,2,1,0:T(8,128)(2,1)S(1)}, bf16[1,1,64,512]{3,2,1,0:T(8,128)(2,1)}, u32[]{:S(2)}) copy-start(bf16[1,1,64,512]{3,2,1,0:T(8,128)(2,1)} %param.16) | copy-start | bytes 196612
  59.4 14.9 %collective-permute-start.7 = (f32[128,512]{1,0:T(8,128)S(1)}, f32[128,512]{1,0:T(8,128)S(1)}, u32[]{:S(2)}, u32[]{:S(2)}) collective-permute-start(f32[128,512]{1,0:T(8,128)S(1)} %get-tuple-element.72), channel_id=1, source_target_pairs={{64,0},{128,64},{192,128},{65,1},{129,65},{193,129},{66,2},{130,66... | collective-permute-start | bytes 786440 | tf_op jit(solution)/shard_map/ppermute | solution.py:33
  71.4 3.4 collective-permute-start.6
  73.0 3.3 copy-start.6
  73.0 3.3 copy-start.10
  74.9 3.0 copy-start.7
  76.2 1.6 copy-start.12
  77.9 2.6 copy-start.4
  77.9 2.6 copy-start.19
  82.0 1.4 copy-start.3
  82.0 2.7 copy-start.2
  83.4 2.2 copy-start.8
  83.4 3.2 copy-start.14
Sparse Core Ops, SparseCore 0:
  82.2 282.1 all-reduce.1
where the time goes:
time: 377 us; the launch traced here: 375 us
  waiting for transfers between devices  297 us (79%)
  matrix products  23.1 us (6%)
  starting transfers between devices  22.7 us (6%)
  between operations  15.1 us (4%)
  other arithmetic  9.13 us (2%)
  local copies, waits for them, and re-layouts  7.76 us (2%)
    psum x1, waiting for transfers between devices, shards(): summed = lax.psum(weight_terms, ('lat', 'lon'))  277 us
    ppermute x2, starting transfers between devices, passed_along(): lax.ppermute(value, axis, [(source, source + steps) for source in range(l...  13.3 us
    ppermute x2, waiting for transfers between devices, shifted(): return lax.ppermute(block, axis, route)  11.4 us
    dot_general x8, matrix products, transpose_product(): lax.dot_general(left_rows, right_rows, (((0,), (0,)), ((), ())), preferre...  9.06 us
  transfers between devices with their start and end apart: 9, of which 7 were waited for; matrix products, arithmetic and copies ran while one was open for 2% of the time, Pallas kernels for 0%

commit v1 on v0

v1 whole, which is shorter than its diff:
```python
import math

import jax
import jax.numpy as jnp
from jax import lax
from jax.experimental import pallas as pl
from jax.experimental.pallas import tpu as pltpu
from jax.sharding import PartitionSpec as P

BF16 = jnp.bfloat16
F32 = jnp.float32
I32 = jnp.int32
MESH = pl.DeviceIdType.MESH
D = 512
GRID = 128
NODES = 64
SLOTS = 9
EXT = SLOTS * NODES


def dot(a, b):
    return lax.dot_general(a, b, (((1,), (0,)), ((), ())), preferred_element_type=F32)


def dot_bt(a, b):
    return lax.dot_general(a, b, (((1,), (1,)), ((), ())), preferred_element_type=F32)


def dot_at(a, b):
    return lax.dot_general(a, b, (((0,), (0,)), ((), ())), preferred_element_type=F32)


def pick_rows(index_row, rows):
    return jnp.where(lax.broadcasted_iota(I32, (rows, 128), 0) == index_row, 1.0, 0.0).astype(BF16)


def pick_cols(index_row, columns):
    turned = jnp.transpose(jnp.broadcast_to(index_row, (128, 128)))
    lane = lax.broadcasted_iota(I32, (128, 128), 1)
    parts = []
    for start in range(0, columns, 128):
        part = jnp.where(turned == lane + start, 1.0, 0.0).astype(BF16)
        parts.append(part[:, : min(128, columns - start)])
    return parts[0] if len(parts) == 1 else jnp.concatenate(parts, 1)


def kernel(
    grid_ref,
    cot_ref,
    mesh_ref,
    mcot_ref,
    proc_ref,
    encw_ref,
    decw_ref,
    index_ref,
    grid_out,
    mesh_out,
    proc_out,
    enc_out,
    dec_out,
    wts,
    gall,
    call,
    mext,
    text,
    town,
    ibuf,
    gproj,
    mproj,
    gpart,
    back,
    hid,
    msg,
    pgrad,
    part,
    gsum,
    gboth,
    fold,
    dwbuf,
    send1,
    recv1,
    send2,
    recv2,
    send3,
    recv3,
    final,
    w_sem,
    own_sem,
    i_sem,
    g_sem,
    c_sem,
    m_sem,
    t_sem,
    f_sem,
    gs_sem,
    r1_sem,
    r2_sem,
    r3_sem,
    r4_sem,
    hs_sem,
    ss_sem,
    fs_sem,
    s1_sem,
    s2_sem,
    s3_sem,
    s4_sem,
    grad_scale,
):
    lat = lax.axis_index("lat")
    lon = lax.axis_index("lon")
    yh = lax.div(lat, 2)
    core = lax.rem(lat, 2)
    z = lax.div(lon, 8)
    yl = lax.rem(lax.div(lon, 4), 2)
    x = lax.rem(lon, 4)
    y = yh * 2 + yl
    sib = (yh * 2 + (1 - core), lon)
    adjacent = core == 1 - yh

    def lon_of(zz, yy, xx):
        return zz * 8 + yy * 4 + xx

    def sector(step):
        return lax.rem(lon + step + 64, 64)

    def x_dev(xx):
        return (lat, lon_of(z, yl, xx))

    def y_dev(yy):
        return (lax.div(yy, 2) * 2 + core, lon_of(z, lax.rem(yy, 2), x))

    def z_dev(zz):
        return (lat, lon_of(zz, yl, x))

    def rcopy(src, dst, ssem, rsem, dev):
        return pltpu.make_async_remote_copy(
            src_ref=src, dst_ref=dst, send_sem=ssem, recv_sem=rsem, device_id=dev, device_id_type=MESH
        )

    def arrived(dst, rsem):
        pltpu.make_async_copy(dst, dst, rsem).wait()

    def load(src, dst, sem):
        pltpu.make_async_copy(src, dst, sem).start()

    load(encw_ref.at[0], wts.at[0], w_sem.at[0])
    load(decw_ref.at[1], wts.at[3], w_sem.at[3])
    load(encw_ref.at[1], wts.at[1], w_sem.at[1])
    load(decw_ref.at[0], wts.at[2], w_sem.at[2])

    @pl.when(core == 0)
    def _():
        load(encw_ref.at[2], wts.at[4], w_sem.at[4])
        load(index_ref.at[pl.ds(0, 8)], ibuf.at[0], i_sem.at[0])
        load(mesh_ref, mext.at[pl.ds(pl.multiple_of((yh * 3 + 1) * NODES, NODES), NODES)], m_sem.at[yh * 3 + 1])
        load(mcot_ref, text.at[pl.ds(pl.multiple_of((yh * 3 + 1) * NODES, NODES), NODES)], t_sem.at[yh * 3 + 1])

    @pl.when(core == 1)
    def _():
        load(decw_ref.at[2], wts.at[4], w_sem.at[4])
        load(index_ref.at[pl.ds(8, 8)], ibuf.at[1], i_sem.at[1])
        slot = (yh + 1) * 3 + 1
        load(proc_ref, mext.at[pl.ds(pl.multiple_of(slot * NODES, NODES), NODES)], m_sem.at[slot])

    own_rows = pl.ds(pl.multiple_of(core * GRID, GRID), GRID)
    load(grid_ref, gall.at[own_rows], g_sem.at[core])
    load(cot_ref, call.at[own_rows], c_sem.at[core])
    load(mcot_ref, town, own_sem)

    barrier = pltpu.get_barrier_semaphore()
    greeted = []
    for dyh in (0, 1):
        for dc in (0, 1):
            for step in (-1, 0, 1):
                if (dyh, dc, step) != (0, 0, 0):
                    to_yh = yh if dyh == 0 else 1 - yh
                    to_core = core if dc == 0 else 1 - core
                    greeted.append((to_yh * 2 + to_core, sector(step)))
    for step in range(1, 4):
        greeted.append(x_dev(lax.rem(x + step, 4)))
        greeted.append(y_dev(lax.rem(y + step, 4)))
    for step in range(1, 8):
        greeted.append(z_dev(lax.rem(z + step, 8)))
    for dev in greeted:
        pl.semaphore_signal(barrier, inc=1, device_id=dev, device_id_type=MESH)
    pl.semaphore_wait(barrier, len(greeted))

    def halo_copies(side, step):
        to_yh = yh if side == 0 else 1 - yh
        slot = (lat - to_yh) * 3 + 1 - step
        rows = pl.ds(pl.multiple_of(slot * NODES, NODES), NODES)
        at = side * 9 + (step + 1) * 3
        enc_dev = (to_yh * 2, sector(step))
        dec_dev = (to_yh * 2 + 1, sector(step))
        return (
            rcopy(mesh_ref, mext.at[rows], hs_sem.at[at], m_sem.at[slot], enc_dev),
            rcopy(mcot_ref, text.at[rows], hs_sem.at[at + 1], t_sem.at[slot], enc_dev),
            rcopy(proc_ref, mext.at[rows], hs_sem.at[at + 2], m_sem.at[slot], dec_dev),
        )

    def each_halo(action):
        @pl.when(adjacent)
        def _():
            for step in (0, 1, -1):
                for copy in halo_copies(1, step):
                    action(copy)

        for step in (1, -1):
            for copy in halo_copies(0, step):
                action(copy)

        to_mesh, to_mcot, to_proc = halo_copies(0, 0)

        @pl.when(core == 0)
        def _():
            action(to_proc)

        @pl.when(core == 1)
        def _():
            action(to_mesh)
            action(to_mcot)

    def each_swap(action):
        action(rcopy(grid_ref, gall.at[own_rows], ss_sem.at[0], g_sem.at[core], sib))

        @pl.when(core == 0)
        def _():
            action(rcopy(index_ref.at[pl.ds(8, 8)], ibuf.at[0], ss_sem.at[1], i_sem.at[0], sib))
            action(rcopy(cot_ref, call.at[pl.ds(0, GRID)], ss_sem.at[2], c_sem.at[0], sib))

        @pl.when(core == 1)
        def _():
            action(rcopy(index_ref.at[pl.ds(0, 8)], ibuf.at[1], ss_sem.at[1], i_sem.at[1], sib))

    each_swap(lambda copy: copy.start())
    each_halo(lambda copy: copy.start())

    @pl.when(jnp.logical_not(adjacent))
    def _():
        for role in (0, 1):
            for k in (3, 4, 5):
                fold[role, k] = jnp.zeros((NODES, D), BF16)

    def stage1_copies(mat, half):
        copies = []
        for step in (1, 3, 2):
            if half == 0:
                to = lax.rem(x + step, 4)
                dev = x_dev(to)
            else:
                to = lax.rem(y + step, 4)
                dev = y_dev(to)
            sem = (mat * 2 + half) * 3 + step - 1
            copies.append(
                rcopy(send1.at[mat, half, to], recv1.at[mat, half, step - 1], s1_sem.at[sem], r1_sem.at[sem], dev)
            )
        return copies

    def stage2_copies(mat, half):
        copies = []
        for step in (1, 3, 2):
            if half == 0:
                to = lax.rem(y + step, 4)
                dev = y_dev(to)
            else:
                to = lax.rem(x + step, 4)
                dev = x_dev(to)
            sem = (mat * 2 + half) * 3 + step - 1
            copies.append(
                rcopy(send2.at[mat, half, to], recv2.at[mat, half, step - 1], s2_sem.at[sem], r2_sem.at[sem], dev)
            )
        return copies

    def send_matrix(mat):
        for xx in range(4):
            pieces = []
            for yy in range(4):
                for zz in range(4):
                    row = ((yy // 2) * 4 + zz) * 64 + (yy % 2) * 32 + xx * 8
                    pieces.append(dwbuf[row : row + 8, 0:256])
            send1[mat, 0, xx] = jnp.concatenate(pieces, 0).astype(BF16)
        for yy in range(4):
            pieces = []
            for xx in range(4):
                for zz in range(4):
                    row = ((yy // 2) * 4 + zz) * 64 + (yy % 2) * 32 + xx * 8
                    pieces.append(dwbuf[row : row + 8, 256:512])
            send1[mat, 1, yy] = jnp.concatenate(pieces, 0).astype(BF16)
        for half in (0, 1):
            for copy in stage1_copies(mat, half):
                copy.start()

    def fold_copies(k_side, step):
        if k_side == 0:
            out = []
            for to_core in (0, 1):
                slot = (yh + to_core) * 3 + 1 + step
                out.append((to_core, slot, (yh * 2 + to_core, sector(step))))
        else:
            slot = (2 - 2 * yh) * 3 + 1 + step
            out = [(2, slot, ((1 - yh) * 2 + yh, sector(step)))]
        copies = []
        for which, slot, dev in out:
            rows = pl.ds(pl.multiple_of(slot * NODES, NODES), NODES)
            k = k_side * 3 + 1 - step
            copies.append(
                rcopy(part.at[rows], fold.at[core, k], fs_sem.at[which * 3 + step + 1], f_sem.at[core * 6 + k], dev)
            )
        return copies

    def each_fold(action):
        for step in (0, 1, -1):
            for copy in fold_copies(1, step):
                action(copy)
        for step in (1, -1):
            for copy in fold_copies(0, step):
                action(copy)
        to_first, to_second = fold_copies(0, 0)

        @pl.when(core == 0)
        def _():
            action(to_second)

        @pl.when(core == 1)
        def _():
            action(to_first)

    def gsum_copy():
        other = pl.ds(pl.multiple_of((1 - core) * GRID, GRID), GRID)
        return rcopy(gsum.at[other], gboth.at[core], ss_sem.at[3], gs_sem, sib)

    def weight(k):
        pltpu.make_async_copy(wts.at[k], wts.at[k], w_sem.at[k]).wait()

    def wait_band(band, with_cot):
        for col in range(3):
            slot = band * 3 + col
            rows = pl.ds(pl.multiple_of(slot * NODES, NODES), NODES)
            arrived(mext.at[rows], m_sem.at[slot])

    def wait_cot(band):
        for col in range(3):
            slot = band * 3 + col
            rows = pl.ds(pl.multiple_of(slot * NODES, NODES), NODES)
            arrived(text.at[rows], t_sem.at[slot])

    def network(role):
        blocks = 2 if role == 0 else 3
        edges = blocks * 128
        w_grid, w_mesh = (0, 1) if role == 0 else (3, 2)
        for band in (0, 1):
            arrived(gall.at[pl.ds(band * GRID, GRID)], g_sem.at[band])
        weight(w_grid)
        gproj[...] = dot(gall[...], wts[w_grid]).astype(BF16)
        for band in (0, 1):
            arrived(ibuf.at[band], i_sem.at[band])
        index = [ibuf[band] for band in (0, 1)]
        grid_rows = [[index[b][(0 if role == 0 else 3) + q : (0 if role == 0 else 3) + q + 1] for q in range(blocks)] for b in (0, 1)]
        shift = [192 * (yh + b - 1) for b in (0, 1)]
        mesh_rows = [
            [index[b][(2 if role == 0 else 0) + q : (2 if role == 0 else 0) + q + 1] + shift[b] for q in range(blocks)]
            for b in (0, 1)
        ]
        weight(4)
        for b in (0, 1):
            rows = slice(b * edges, (b + 1) * edges)
            g_pick = jnp.concatenate([pick_cols(r, GRID) for r in grid_rows[b]], 0)
            gpart[rows] = dot(g_pick, gproj[b * GRID : (b + 1) * GRID])
            if role == 1:
                arrived(call.at[pl.ds(b * GRID, GRID)], c_sem.at[b])
                picked = dot(g_pick, call[b * GRID : (b + 1) * GRID]).astype(BF16)
                msg[rows] = picked
                back[rows] = dot_bt(picked, wts[4])
        weight(w_mesh)
        for k in (0, 1, 2):
            band = (yh + k if k < 2 else 2 - 2 * yh)
            wait_band(band, role == 0)
            rows = pl.ds(pl.multiple_of(band * 192, 192), 192)
            mproj[rows] = dot(mext[rows], wts[w_mesh]).astype(BF16)
        if role == 0:
            for band in range(3):
                wait_cot(band)
        for b in (0, 1):
            rows = slice(b * edges, (b + 1) * edges)
            m_pick = jnp.concatenate([pick_cols(r, EXT) for r in mesh_rows[b]], 0)
            pre = dot(m_pick, mproj[...]) + gpart[rows]
            if role == 0:
                place = lax.broadcasted_iota(I32, (edges, D), 0)
                live = index[b][4:5, 0:1]
                picked = jnp.where(place < live, dot(m_pick, text[...]), 0.0).astype(BF16)
                msg[rows] = picked
                grown = dot_bt(picked, wts[4])
            else:
                grown = back[rows]
            gate = 1.0 / (1.0 + jnp.exp(-pre))
            hid[rows] = (pre * gate).astype(BF16)
            pgrad[rows] = (grown * (gate * (1.0 + pre * (1.0 - gate)))).astype(BF16)
        every = slice(0, 2 * edges)
        dwbuf[...] = dot_at(hid[every], msg[every])
        send_matrix(2)
        m_turn = jnp.concatenate([pick_rows(r, EXT) for b in (0, 1) for r in mesh_rows[b]], 1)
        part[...] = dot(m_turn, pgrad[every]).astype(BF16)
        each_fold(lambda copy: copy.start())
        dwbuf[...] = dot_at(mext[...], part[...])
        send_matrix(1 if role == 0 else 0)
        for b in (0, 1):
            g_turn = jnp.concatenate([pick_rows(r, GRID) for r in grid_rows[b]], 1)
            gsum[b * GRID : (b + 1) * GRID] = dot(g_turn, pgrad[b * edges : (b + 1) * edges]).astype(BF16)
        gsum_copy().start()
        dwbuf[...] = dot_at(gall[...], gsum[...])
        send_matrix(0 if role == 0 else 1)

    @pl.when(core == 0)
    def _():
        network(0)

    @pl.when(core == 1)
    def _():
        network(1)

    @pl.when(core == 0)
    def _():
        for k in (2, 3):
            weight(k)
        arrived(call.at[own_rows], c_sem.at[0])

    @pl.when(core == 1)
    def _():
        for k in (0, 1):
            weight(k)

    arrived(town, own_sem)

    for mat in (2, 0, 1):
        for half in (0, 1):
            for step in range(3):
                sem = (mat * 2 + half) * 3 + step
                arrived(recv1.at[mat, half, step], r1_sem.at[sem])
            own = x if half == 0 else y
            total = send1[mat, half, own].astype(F32)
            for step in range(3):
                total = total + recv1[mat, half, step].astype(F32)
            total = total.astype(BF16)
            for k in range(4):
                send2[mat, half, k] = total[k * 32 : (k + 1) * 32]
            for copy in stage2_copies(mat, half):
                copy.start()

    gboth[core] = gsum[own_rows]
    arrived(gboth.at[1 - core], gs_sem)
    grid_out[...] = (call[own_rows].astype(F32) + dot_bt(gboth[0], wts[0]) + dot_bt(gboth[1], wts[3])).astype(BF16)

    sums = []
    for mat in range(3):
        for half in (0, 1):
            for step in range(3):
                sem = (mat * 2 + half) * 3 + step
                arrived(recv2.at[mat, half, step], r2_sem.at[sem])
            own = y if half == 0 else x
            total = send2[mat, half, own].astype(F32)
            for step in range(3):
                total = total + recv2[mat, half, step].astype(F32)
            sums.append(total)
    for q in range(4):
        send3[q] = jnp.concatenate([s[q * 8 : (q + 1) * 8] for s in sums], 0).astype(BF16)

    holds = lax.div(z, 4) == yh

    def stage3_copy(step):
        to = lax.rem(z + step, 8)
        return (
            lax.div(to, 4) == yh,
            rcopy(send3.at[lax.rem(to, 4)], recv3.at[step - 1], s3_sem.at[step - 1], r3_sem.at[step - 1], z_dev(to)),
        )

    for step in (4, 3, 5, 2, 6, 1, 7):
        goes, copy = stage3_copy(step)
        pl.when(goes)(copy.start)

    def fold_wait(role, k):
        arrived(fold.at[role, k], f_sem.at[role * 6 + k])

    for role in (0, 1):
        for k in (0, 2):
            fold_wait(role, k)
    own_slot = pl.ds(pl.multiple_of(((yh + core) * 3 + 1) * NODES, NODES), NODES)

    @pl.when(core == 0)
    def _():
        fold_wait(1, 1)
        fold[0, 1] = part[own_slot]

    @pl.when(core == 1)
    def _():
        fold_wait(0, 1)
        fold[1, 1] = part[own_slot]

    @pl.when(adjacent)
    def _():
        for role in (0, 1):
            for k in (3, 4, 5):
                fold_wait(role, k)

    def folded(role):
        total = fold[role, 0].astype(F32)
        for k in range(1, 6):
            total = total + fold[role, k].astype(F32)
        return total.astype(BF16)

    mesh_out[...] = (town[...].astype(F32) + dot_bt(folded(0), wts[1])).astype(BF16)
    proc_out[...] = dot_bt(folded(1), wts[2]).astype(BF16)

    def last_copies():
        return (
            rcopy(final.at[core], final.at[core], s4_sem.at[0], r4_sem.at[core], sib),
            rcopy(final.at[core], final.at[core], s4_sem.at[1], r4_sem.at[core], ((1 - yh) * 2 + core, lon)),
            rcopy(final.at[core], final.at[core], s4_sem.at[2], r4_sem.at[core], ((1 - yh) * 2 + 1 - core, lon)),
        )

    @pl.when(holds)
    def _():
        total = send3[lax.rem(z, 4)].astype(F32)
        for step in (1, 7, 2, 6, 3, 5, 4):
            arrived(recv3.at[step - 1], r3_sem.at[step - 1])
            total = total + recv3[step - 1].astype(F32)
        total = total * grad_scale
        pieces = []
        for mat in range(3):
            low = total[mat * 16 : mat * 16 + 8]
            high = total[mat * 16 + 8 : mat * 16 + 16]
            pieces.append(jnp.concatenate([low, high], 1))
        final[core] = jnp.concatenate(pieces, 0)
        for copy in last_copies():
            copy.start()
        arrived(final.at[1 - core], r4_sem.at[1 - core])

    @pl.when(jnp.logical_not(holds))
    def _():
        arrived(final.at[0], r4_sem.at[0])
        arrived(final.at[1], r4_sem.at[1])

    enc_out[...] = final[0]
    dec_out[...] = final[1]

    each_swap(lambda copy: copy.wait_send())
    each_halo(lambda copy: copy.wait_send())
    each_fold(lambda copy: copy.wait_send())
    gsum_copy().wait_send()
    for mat in range(3):
        for half in (0, 1):
            for copy in stage1_copies(mat, half) + stage2_copies(mat, half):
                copy.wait_send()
    for step in range(1, 8):
        goes, copy = stage3_copy(step)
        pl.when(goes)(copy.wait_send)

    @pl.when(holds)
    def _():
        for copy in last_copies():
            copy.wait_send()


def shards(
    grid_latent,
    grid_cot,
    mesh_latent,
    mesh_cot,
    processed,
    enc_weights,
    dec_weights,
    enc_send,
    enc_recv,
    enc_live,
    dec_send,
    dec_recv,
):
    index = jnp.concatenate(
        [
            enc_send[0, 0],
            enc_recv[0, 0],
            jnp.broadcast_to(enc_live[0], (4, 128)),
            dec_send[0, 0],
            dec_recv[0, 0],
            jnp.zeros((2, 128), I32),
        ],
        0,
    )
    grad_scale = 1.0 / math.sqrt(4 * 64 * 128)
    vmem = pltpu.VMEM
    dma = pltpu.SemaphoreType.DMA
    outs = pl.pallas_call(
        lambda *refs: kernel(*refs, grad_scale),
        out_shape=(
            jax.ShapeDtypeStruct((GRID, D), BF16),
            jax.ShapeDtypeStruct((NODES, D), BF16),
            jax.ShapeDtypeStruct((NODES, D), BF16),
            jax.ShapeDtypeStruct((24, D), F32),
            jax.ShapeDtypeStruct((24, D), F32),
        ),
        in_specs=[pl.BlockSpec(memory_space=pl.ANY)] * 8,
        out_specs=(pl.BlockSpec(memory_space=pltpu.VMEM),) * 5,
        scratch_shapes=[
            vmem((5, D, D), BF16),
            vmem((2 * GRID, D), BF16),
            vmem((2 * GRID, D), BF16),
            vmem((EXT, D), BF16),
            vmem((EXT, D), BF16),
            vmem((NODES, D), BF16),
            vmem((2, 8, 128), I32),
            vmem((2 * GRID, D), BF16),
            vmem((EXT, D), BF16),
            vmem((768, D), F32),
            vmem((768, D), F32),
            vmem((768, D), BF16),
            vmem((768, D), BF16),
            vmem((768, D), BF16),
            vmem((EXT, D), BF16),
            vmem((2 * GRID, D), BF16),
            vmem((2, GRID, D), BF16),
            vmem((2, 6, NODES, D), BF16),
            vmem((D, D), F32),
            vmem((3, 2, 4, 128, 256), BF16),
            vmem((3, 2, 3, 128, 256), BF16),
            vmem((3, 2, 4, 32, 256), BF16),
            vmem((3, 2, 3, 32, 256), BF16),
            vmem((4, 48, 256), BF16),
            vmem((7, 48, 256), BF16),
            vmem((2, 24, D), F32),
            dma((5,)),
            dma,
            dma((2,)),
            dma((2,)),
            dma((2,)),
            dma((9,)),
            dma((9,)),
            dma((12,)),
            dma,
            dma((18,)),
            dma((18,)),
            dma((7,)),
            dma((2,)),
            dma((18,)),
            dma((4,)),
            dma((9,)),
            dma((18,)),
            dma((18,)),
            dma((7,)),
            dma((3,)),
        ],
        compiler_params=pltpu.CompilerParams(
            collective_id=0, has_side_effects=True, vmem_limit_bytes=48 * 2**20
        ),
        name="edge_layer",
    )(
        grid_latent[0, 0],
        grid_cot[0, 0],
        mesh_latent[0, 0],
        mesh_cot[0, 0],
        processed[0, 0],
        enc_weights,
        dec_weights,
        index,
    )
    grid_grad, mesh_grad, proc_grad, enc_grads, dec_grads = outs
    return (
        grid_grad[None, None],
        mesh_grad[None, None],
        proc_grad[None, None],
        enc_grads.reshape(3, 8, D),
        dec_grads.reshape(3, 8, D),
    )


def solution(mesh):
    by_node = P("lat", "lon", None, None)
    return jax.shard_map(
        shards,
        mesh=mesh,
        in_specs=(by_node,) * 5 + (P(), P()) + (by_node, by_node, P("lat", "lon", None), by_node, by_node),
        out_specs=(by_node, by_node, by_node, P(None, "lon", None), P(None, "lon", None)),
        check_vma=False,
    )
```

time: 377 us -> 67.3 us (0.18)
  waiting for transfers between devices: 297 us -> 0 us
  Pallas kernels: 0 us -> 53.9 us
  matrix products: 23.1 us -> 0 us
  starting transfers between devices: 22.7 us -> 0 us
  between operations: 15.1 us -> 1.3 us
  other arithmetic: 9.13 us -> 0 us
  local copies, waits for them, and re-layouts: 7.76 us -> 11.7 us
    psum x1 -> x0, waiting for transfers between devices: 277 us -> none  [shards(): summed = lax.psum(weight_terms, ('lat', 'lon'))]
    pallas_call x0 -> x1, Pallas kernels: none -> 53.9 us  [shards(): pl.pallas_call(lambda *refs: kernel(*refs, grad_scale), out_shape=(jax.Sh...]
    dot_general x19 -> x0, matrix products: 23.1 us -> none  [the longest x8 9.06 us: transpose_product(): lax.dot_general(left_rows, right_rows, (((0,), (0,)), ((), ())), preferre...]
    ppermute x8 -> x0, starting transfers between devices: 22.7 us -> none  [the longest x2 13.3 us: passed_along(): lax.ppermute(value, axis, [(source, source + steps) for source in range(l...]
    ppermute x8 -> x0, waiting for transfers between devices: 20.2 us -> none  [the longest x2 11.4 us: shifted(): return lax.ppermute(block, axis, route)]
    unnamed x42 -> x20, local copies, waits for them, and re-layouts: 3.18 us -> 11 us
    scatter-add x2 -> x0, other arithmetic: 5.57 us -> none  [the longest x1 3.17 us: dec_step(): jax.ops.segment_sum(pre_grad.astype(jnp.float32), senders, num_segments=e...]
    gather x3 -> x0, local copies, waits for them, and re-layouts: 4.37 us -> none  [the longest x1 2.06 us: dec_step(): jnp.take(proc_ext, senders, axis=0).astype(jnp.float32)]
  transfers between devices with their start and end apart: 9 -> 0, of which waited for: 7 -> 0; matrix products, arithmetic and copies ran while one was open for 2% -> 0% of each run, Pallas kernels for 0% -> 0%
where the time goes in v1:
time: 67.3 us; the launch traced here: 67 us
  Pallas kernels  53.9 us (80%)
  local copies, waits for them, and re-layouts  11.7 us (17%)
  between operations  1.3 us (2%)
    pallas_call x1, Pallas kernels, shards(): pl.pallas_call(lambda *refs: kernel(*refs, grad_scale), out_shape=(jax.Sh...  53.9 us
    unnamed x20, local copies, waits for them, and re-layouts  11 us

profile of v1, /device:TPU:25, one launch (start us, length us, event | category | flops | bytes accessed | tf_op | source)
XLA Modules:
  0.0 67.0 jit_solution(3191280676734709613)
XLA Ops:
  1.3 0.7 %copy_bitcast_fusion = (s32[3,128]{1,0:T(4,128)S(1)}, s32[3,128]{1,0:T(4,128)S(1)}) fusion(s32[1,1,3,128]{3,1,2,0:T(1,128)} %param.23, s32[1,1,3,128]{3,1,2,0:T(1,128)} %param.22), kind=kLoop, calls=%fused_computation | loop fusion | bytes 6144
  2.0 0.7 %concatenate.3.refs_7_ = s32[16,128]{1,0:T(8,128)S(1)} concatenate(s32[2,128]{1,0:T(2,128)} %bitcast.28, s32[2,128]{1,0:T(2,128)} %bitcast.29, s32[4,128]{1,0:T(4,128)S(1)} %broadcast_in_dim.20, s32[3,128]{1,0:T(4,128)S(1)} %get-tuple-element.16, s32[3,128]{1,0:T(4,128)S(1)} %get-tuple-element.15, s32[2,128]{1,0:T(2,128)S(1)} %broadcast_in_dim.21), dimensions={0} | concatenate | bytes 16384 | tf_op jit(solution)/shard_map/concatenate | solution.py:577
  2.7 0.0 copy-start
  2.7 1.4 %copy-done = bf16[3,512,512]{2,1,0:T(8,128)(2,1)S(1)} copy-done((bf16[3,512,512]{2,1,0:T(8,128)(2,1)S(1)}, bf16[3,512,512]{2,1,0:T(8,128)(2,1)}, u32[]{:S(2)}) %copy-start) | copy-done | bytes 1572888
  4.1 0.0 copy-start.1
  4.1 1.4 %copy-done.1 = bf16[3,512,512]{2,1,0:T(8,128)(2,1)S(1)} copy-done((bf16[3,512,512]{2,1,0:T(8,128)(2,1)S(1)}, bf16[3,512,512]{2,1,0:T(8,128)(2,1)}, u32[]{:S(2)}) %copy-start.1) | copy-done | bytes 1572888
  5.5 0.0 copy-start.2
  5.5 0.9 %copy-done.2 = bf16[1,1,128,512]{3,2,1,0:T(8,128)(2,1)S(1)} copy-done((bf16[1,1,128,512]{3,2,1,0:T(8,128)(2,1)S(1)}, bf16[1,1,128,512]{3,2,1,0:T(8,128)(2,1)}, u32[]{:S(2)}) %copy-start.2) | copy-done | bytes 131096
  6.4 0.0 copy-start.3
  6.4 0.9 %copy-done.3 = bf16[1,1,128,512]{3,2,1,0:T(8,128)(2,1)S(1)} copy-done((bf16[1,1,128,512]{3,2,1,0:T(8,128)(2,1)S(1)}, bf16[1,1,128,512]{3,2,1,0:T(8,128)(2,1)}, u32[]{:S(2)}) %copy-start.3) | copy-done | bytes 131096
  7.3 0.0 copy-start.4
  7.4 0.8 %copy-done.4 = bf16[1,1,64,512]{3,2,1,0:T(8,128)(2,1)S(1)} copy-done((bf16[1,1,64,512]{3,2,1,0:T(8,128)(2,1)S(1)}, bf16[1,1,64,512]{3,2,1,0:T(8,128)(2,1)}, u32[]{:S(2)}) %copy-start.4) | copy-done | bytes 65560
  8.2 0.0 copy-start.5
  8.2 0.8 %copy-done.5 = bf16[1,1,64,512]{3,2,1,0:T(8,128)(2,1)S(1)} copy-done((bf16[1,1,64,512]{3,2,1,0:T(8,128)(2,1)S(1)}, bf16[1,1,64,512]{3,2,1,0:T(8,128)(2,1)}, u32[]{:S(2)}) %copy-start.5) | copy-done | bytes 65560
  9.0 0.0 copy-start.6
  9.0 0.8 %copy-done.6 = bf16[1,1,64,512]{3,2,1,0:T(8,128)(2,1)S(1)} copy-done((bf16[1,1,64,512]{3,2,1,0:T(8,128)(2,1)S(1)}, bf16[1,1,64,512]{3,2,1,0:T(8,128)(2,1)}, u32[]{:S(2)}) %copy-start.6) | copy-done | bytes 65560
  9.9 53.9 %edge_layer.1 = (bf16[128,512]{1,0:T(8,128)(2,1)S(1)}, bf16[64,512]{1,0:T(8,128)(2,1)S(1)}, bf16[64,512]{1,0:T(8,128)(2,1)S(1)}, f32[24,512]{1,0:T(8,128)S(1)}, f32[24,512]{1,0:T(8,128)S(1)}) custom-call(bf16[128,512]{1,0:T(8,128)(2,1)S(1)} %bitcast.18, bf16[128,512]{1,0:T(8,128)(2,1)S(1)} %bitcast.19, bf16[64,512]{1,0:T(8,128)(2,1)S(1)} %bitcast.21, ...), custom_call_target="tpu_custom_call" | custom-call | tf_op jit(solution)/shard_map/edge_layer/pallas_call | solution.py:591
  63.8 0.7 copy.27
  64.5 0.6 copy.28
  65.1 0.6 copy.29
  65.7 0.6 copy.30
  66.3 0.6 copy.31
  (2 shorter events, 0.0 us)
Async XLA Ops:
  2.7 1.4 %copy-start = (bf16[3,512,512]{2,1,0:T(8,128)(2,1)S(1)}, bf16[3,512,512]{2,1,0:T(8,128)(2,1)}, u32[]{:S(2)}) copy-start(bf16[3,512,512]{2,1,0:T(8,128)(2,1)} %refs_5_.1) | copy-start | bytes 4718596
  4.1 1.4 %copy-start.1 = (bf16[3,512,512]{2,1,0:T(8,128)(2,1)S(1)}, bf16[3,512,512]{2,1,0:T(8,128)(2,1)}, u32[]{:S(2)}) copy-start(bf16[3,512,512]{2,1,0:T(8,128)(2,1)} %refs_6_.1) | copy-start | bytes 4718596
  5.5 0.9 %copy-start.2 = (bf16[1,1,128,512]{3,2,1,0:T(8,128)(2,1)S(1)}, bf16[1,1,128,512]{3,2,1,0:T(8,128)(2,1)}, u32[]{:S(2)}) copy-start(bf16[1,1,128,512]{3,2,1,0:T(8,128)(2,1)} %param.12) | copy-start | bytes 393220
  6.4 0.9 %copy-start.3 = (bf16[1,1,128,512]{3,2,1,0:T(8,128)(2,1)S(1)}, bf16[1,1,128,512]{3,2,1,0:T(8,128)(2,1)}, u32[]{:S(2)}) copy-start(bf16[1,1,128,512]{3,2,1,0:T(8,128)(2,1)} %param.13) | copy-start | bytes 393220
  7.3 0.8 %copy-start.4 = (bf16[1,1,64,512]{3,2,1,0:T(8,128)(2,1)S(1)}, bf16[1,1,64,512]{3,2,1,0:T(8,128)(2,1)}, u32[]{:S(2)}) copy-start(bf16[1,1,64,512]{3,2,1,0:T(8,128)(2,1)} %param.14) | copy-start | bytes 196612
  8.2 0.8 %copy-start.5 = (bf16[1,1,64,512]{3,2,1,0:T(8,128)(2,1)S(1)}, bf16[1,1,64,512]{3,2,1,0:T(8,128)(2,1)}, u32[]{:S(2)}) copy-start(bf16[1,1,64,512]{3,2,1,0:T(8,128)(2,1)} %param.15) | copy-start | bytes 196612
  9.0 0.8 %copy-start.6 = (bf16[1,1,64,512]{3,2,1,0:T(8,128)(2,1)S(1)}, bf16[1,1,64,512]{3,2,1,0:T(8,128)(2,1)}, u32[]{:S(2)}) copy-start(bf16[1,1,64,512]{3,2,1,0:T(8,128)(2,1)} %param.16) | copy-start | bytes 196612

commit v2 on v1

--- a/solution.py
+++ b/solution.py
@@ -52,19 +52,25 @@
     proc_ref,
     encw_ref,
     decw_ref,
-    index_ref,
+    esend_ref,
+    erecv_ref,
+    live_ref,
+    dsend_ref,
+    drecv_ref,
     grid_out,
     mesh_out,
     proc_out,
-    enc_out,
-    dec_out,
+    weights_out,
     wts,
     gall,
     call,
     mext,
     text,
     town,
-    ibuf,
+    ebuf,
+    dbuf,
+    lbuf,
+    lone,
     gproj,
     mproj,
     gpart,
@@ -151,21 +157,24 @@
     @pl.when(core == 0)
     def _():
         load(encw_ref.at[2], wts.at[4], w_sem.at[4])
-        load(index_ref.at[pl.ds(0, 8)], ibuf.at[0], i_sem.at[0])
+        load(esend_ref, ebuf.at[0, 0], i_sem.at[0])
+        load(erecv_ref, ebuf.at[0, 1], i_sem.at[1])
         load(mesh_ref, mext.at[pl.ds(pl.multiple_of((yh * 3 + 1) * NODES, NODES), NODES)], m_sem.at[yh * 3 + 1])
         load(mcot_ref, text.at[pl.ds(pl.multiple_of((yh * 3 + 1) * NODES, NODES), NODES)], t_sem.at[yh * 3 + 1])
 
     @pl.when(core == 1)
     def _():
         load(decw_ref.at[2], wts.at[4], w_sem.at[4])
-        load(index_ref.at[pl.ds(8, 8)], ibuf.at[1], i_sem.at[1])
+        load(dsend_ref, dbuf.at[1, 0], i_sem.at[2])
+        load(drecv_ref, dbuf.at[1, 1], i_sem.at[3])
         slot = (yh + 1) * 3 + 1
         load(proc_ref, mext.at[pl.ds(pl.multiple_of(slot * NODES, NODES), NODES)], m_sem.at[slot])
 
     own_rows = pl.ds(pl.multiple_of(core * GRID, GRID), GRID)
     load(grid_ref, gall.at[own_rows], g_sem.at[core])
     load(cot_ref, call.at[own_rows], c_sem.at[core])
-    load(mcot_ref, town, own_sem)
+    load(mcot_ref, town, own_sem.at[0])
+    load(live_ref, lone, own_sem.at[1])
 
     barrier = pltpu.get_barrier_semaphore()
     greeted = []
@@ -198,42 +207,44 @@
             rcopy(proc_ref, mext.at[rows], hs_sem.at[at + 2], m_sem.at[slot], dec_dev),
         )
 
-    def each_halo(action):
+    def each_halo(which, action):
         @pl.when(adjacent)
         def _():
-            for step in (0, 1, -1):
-                for copy in halo_copies(1, step):
-                    action(copy)
+            for step in (1, -1, 0):
+                for w in which:
+                    action(halo_copies(1, step)[w])
 
         for step in (1, -1):
-            for copy in halo_copies(0, step):
-                action(copy)
-
-        to_mesh, to_mcot, to_proc = halo_copies(0, 0)
+            for w in which:
+                action(halo_copies(0, step)[w])
+
+        @pl.when(core == (0 if 2 in which else 1))
+        def _():
+            for w in which:
+                action(halo_copies(0, 0)[w])
+
+    cross_band = 2 - 2 * yh
+
+    def each_swap(action):
+        action(rcopy(grid_ref, gall.at[own_rows], ss_sem.at[0], g_sem.at[core], sib))
 
         @pl.when(core == 0)
         def _():
-            action(to_proc)
+            action(rcopy(dsend_ref, dbuf.at[0, 0], ss_sem.at[1], i_sem.at[0], sib))
+            action(rcopy(drecv_ref, dbuf.at[0, 1], ss_sem.at[4], i_sem.at[1], sib))
+            action(rcopy(cot_ref, call.at[pl.ds(0, GRID)], ss_sem.at[2], c_sem.at[0], sib))
 
         @pl.when(core == 1)
         def _():
-            action(to_mesh)
-            action(to_mcot)
-
-    def each_swap(action):
-        action(rcopy(grid_ref, gall.at[own_rows], ss_sem.at[0], g_sem.at[core], sib))
-
-        @pl.when(core == 0)
-        def _():
-            action(rcopy(index_ref.at[pl.ds(8, 8)], ibuf.at[0], ss_sem.at[1], i_sem.at[0], sib))
-            action(rcopy(cot_ref, call.at[pl.ds(0, GRID)], ss_sem.at[2], c_sem.at[0], sib))
-
-        @pl.when(core == 1)
-        def _():
-            action(rcopy(index_ref.at[pl.ds(0, 8)], ibuf.at[1], ss_sem.at[1], i_sem.at[1], sib))
-
+            action(rcopy(esend_ref, ebuf.at[1, 0], ss_sem.at[1], i_sem.at[2], sib))
+            action(rcopy(erecv_ref, ebuf.at[1, 1], ss_sem.at[4], i_sem.at[3], sib))
+            action(rcopy(lbuf.at[1], lbuf.at[1], ss_sem.at[5], i_sem.at[4], sib))
+
+    each_halo((2,), lambda copy: copy.start())
+    arrived(lone, own_sem.at[1])
+    lbuf[core] = jnp.broadcast_to(lone[0], (8, 128))
     each_swap(lambda copy: copy.start())
-    each_halo(lambda copy: copy.start())
+    each_halo((0, 1), lambda copy: copy.start())
 
     @pl.when(jnp.logical_not(adjacent))
     def _():
@@ -290,28 +301,21 @@
             for copy in stage1_copies(mat, half):
                 copy.start()
 
-    def fold_copies(k_side, step):
-        if k_side == 0:
-            out = []
-            for to_core in (0, 1):
-                slot = (yh + to_core) * 3 + 1 + step
-                out.append((to_core, slot, (yh * 2 + to_core, sector(step))))
-        else:
-            slot = (2 - 2 * yh) * 3 + 1 + step
-            out = [(2, slot, ((1 - yh) * 2 + yh, sector(step)))]
+    def fold_copies(side, step):
         copies = []
-        for which, slot, dev in out:
+        for which in ((0, 1) if side == 0 else (2,)):
+            slot = ((yh + which) if side == 0 else cross_band) * 3 + 1 + step
+            dev = (yh * 2 + which if side == 0 else (1 - yh) * 2 + yh, sector(step))
             rows = pl.ds(pl.multiple_of(slot * NODES, NODES), NODES)
-            k = k_side * 3 + 1 - step
+            k = side * 3 + 1 - step
             copies.append(
                 rcopy(part.at[rows], fold.at[core, k], fs_sem.at[which * 3 + step + 1], f_sem.at[core * 6 + k], dev)
             )
         return copies
 
     def each_fold(action):
-        for step in (0, 1, -1):
-            for copy in fold_copies(1, step):
-                action(copy)
+        for step in (1, -1, 0):
+            action(fold_copies(1, step)[0])
         for step in (1, -1):
             for copy in fold_copies(0, step):
                 action(copy)
@@ -332,7 +336,7 @@
     def weight(k):
         pltpu.make_async_copy(wts.at[k], wts.at[k], w_sem.at[k]).wait()
 
-    def wait_band(band, with_cot):
+    def wait_band(band):
         for col in range(3):
             slot = band * 3 + col
             rows = pl.ds(pl.multiple_of(slot * NODES, NODES), NODES)
@@ -352,15 +356,21 @@
             arrived(gall.at[pl.ds(band * GRID, GRID)], g_sem.at[band])
         weight(w_grid)
         gproj[...] = dot(gall[...], wts[w_grid]).astype(BF16)
+        picks = ebuf if role == 0 else dbuf
         for band in (0, 1):
-            arrived(ibuf.at[band], i_sem.at[band])
-        index = [ibuf[band] for band in (0, 1)]
-        grid_rows = [[index[b][(0 if role == 0 else 3) + q : (0 if role == 0 else 3) + q + 1] for q in range(blocks)] for b in (0, 1)]
-        shift = [192 * (yh + b - 1) for b in (0, 1)]
-        mesh_rows = [
-            [index[b][(2 if role == 0 else 0) + q : (2 if role == 0 else 0) + q + 1] + shift[b] for q in range(blocks)]
-            for b in (0, 1)
-        ]
+            for which in (0, 1):
+                arrived(picks.at[band, which], i_sem.at[band * 2 + which])
+        if role == 0:
+            arrived(lbuf.at[1], i_sem.at[4])
+
+        def rows_of(band, which):
+            if role == 0:
+                both = picks[band, which]
+                return [both[q : q + 1] for q in range(blocks)]
+            return [picks[band, which, q] for q in range(blocks)]
+
+        grid_rows = [rows_of(b, role) for b in (0, 1)]
+        mesh_rows = [[r + 192 * (yh + b - 1) for r in rows_of(b, 1 - role)] for b in (0, 1)]
         weight(4)
         for b in (0, 1):
             rows = slice(b * edges, (b + 1) * edges)
@@ -373,8 +383,8 @@
                 back[rows] = dot_bt(picked, wts[4])
         weight(w_mesh)
         for k in (0, 1, 2):
-            band = (yh + k if k < 2 else 2 - 2 * yh)
-            wait_band(band, role == 0)
+            band = (yh + k if k < 2 else cross_band)
+            wait_band(band)
             rows = pl.ds(pl.multiple_of(band * 192, 192), 192)
             mproj[rows] = dot(mext[rows], wts[w_mesh]).astype(BF16)
         if role == 0:
@@ -386,7 +396,7 @@
             pre = dot(m_pick, mproj[...]) + gpart[rows]
             if role == 0:
                 place = lax.broadcasted_iota(I32, (edges, D), 0)
-                live = index[b][4:5, 0:1]
+                live = lbuf[b, 0:1, 0:1]
                 picked = jnp.where(place < live, dot(m_pick, text[...]), 0.0).astype(BF16)
                 msg[rows] = picked
                 grown = dot_bt(picked, wts[4])
@@ -400,15 +410,18 @@
         send_matrix(2)
         m_turn = jnp.concatenate([pick_rows(r, EXT) for b in (0, 1) for r in mesh_rows[b]], 1)
         part[...] = dot(m_turn, pgrad[every]).astype(BF16)
-        each_fold(lambda copy: copy.start())
-        dwbuf[...] = dot_at(mext[...], part[...])
-        send_matrix(1 if role == 0 else 0)
+        if role == 1:
+            dwbuf[...] = dot_at(mext[...], part[...])
+            send_matrix(0)
         for b in (0, 1):
             g_turn = jnp.concatenate([pick_rows(r, GRID) for r in grid_rows[b]], 1)
             gsum[b * GRID : (b + 1) * GRID] = dot(g_turn, pgrad[b * edges : (b + 1) * edges]).astype(BF16)
         gsum_copy().start()
         dwbuf[...] = dot_at(gall[...], gsum[...])
         send_matrix(0 if role == 0 else 1)
+        if role == 0:
+            dwbuf[...] = dot_at(mext[...], part[...])
+            send_matrix(1)
 
     @pl.when(core == 0)
     def _():
@@ -429,7 +442,7 @@
         for k in (0, 1):
             weight(k)
 
-    arrived(town, own_sem)
+    arrived(town, own_sem.at[0])
 
     for mat in (2, 0, 1):
         for half in (0, 1):
@@ -446,6 +459,8 @@
             for copy in stage2_copies(mat, half):
                 copy.start()
 
+    each_fold(lambda copy: copy.start())
+
     gboth[core] = gsum[own_rows]
     arrived(gboth.at[1 - core], gs_sem)
     grid_out[...] = (call[own_rows].astype(F32) + dot_bt(gboth[0], wts[0]) + dot_bt(gboth[1], wts[3])).astype(BF16)
@@ -477,13 +492,16 @@
         goes, copy = stage3_copy(step)
         pl.when(goes)(copy.start)
 
+    def part_of(slot):
+        return pl.ds(pl.multiple_of(slot * NODES, NODES), NODES)
+
     def fold_wait(role, k):
         arrived(fold.at[role, k], f_sem.at[role * 6 + k])
 
     for role in (0, 1):
         for k in (0, 2):
             fold_wait(role, k)
-    own_slot = pl.ds(pl.multiple_of(((yh + core) * 3 + 1) * NODES, NODES), NODES)
+    own_slot = part_of((yh + core) * 3 + 1)
 
     @pl.when(core == 0)
     def _():
@@ -511,11 +529,8 @@
     proc_out[...] = dot_bt(folded(1), wts[2]).astype(BF16)
 
     def last_copies():
-        return (
-            rcopy(final.at[core], final.at[core], s4_sem.at[0], r4_sem.at[core], sib),
-            rcopy(final.at[core], final.at[core], s4_sem.at[1], r4_sem.at[core], ((1 - yh) * 2 + core, lon)),
-            rcopy(final.at[core], final.at[core], s4_sem.at[2], r4_sem.at[core], ((1 - yh) * 2 + 1 - core, lon)),
-        )
+        devs = (((1 - yh) * 2 + core, lon), ((1 - yh) * 2 + 1 - core, lon), sib)
+        return [rcopy(final.at[core], final.at[core], s4_sem.at[k], r4_sem.at[core], dev) for k, dev in enumerate(devs)]
 
     @pl.when(holds)
     def _():
@@ -523,13 +538,7 @@
         for step in (1, 7, 2, 6, 3, 5, 4):
             arrived(recv3.at[step - 1], r3_sem.at[step - 1])
             total = total + recv3[step - 1].astype(F32)
-        total = total * grad_scale
-        pieces = []
-        for mat in range(3):
-            low = total[mat * 16 : mat * 16 + 8]
-            high = total[mat * 16 + 8 : mat * 16 + 16]
-            pieces.append(jnp.concatenate([low, high], 1))
-        final[core] = jnp.concatenate(pieces, 0)
+        final[core] = (total * grad_scale).astype(BF16)
         for copy in last_copies():
             copy.start()
         arrived(final.at[1 - core], r4_sem.at[1 - core])
@@ -539,12 +548,17 @@
         arrived(final.at[0], r4_sem.at[0])
         arrived(final.at[1], r4_sem.at[1])
 
-    enc_out[...] = final[0]
-    dec_out[...] = final[1]
+    for role in (0, 1):
+        pieces = final[role].astype(F32)
+        for mat in range(3):
+            weights_out[role, mat, :, 0:256] = pieces[mat * 16 : mat * 16 + 8]
+            weights_out[role, mat, :, 256:512] = pieces[mat * 16 + 8 : mat * 16 + 16]
 
     each_swap(lambda copy: copy.wait_send())
-    each_halo(lambda copy: copy.wait_send())
+    each_halo((2,), lambda copy: copy.wait_send())
+    each_halo((0, 1), lambda copy: copy.wait_send())
     each_fold(lambda copy: copy.wait_send())
+
     gsum_copy().wait_send()
     for mat in range(3):
         for half in (0, 1):
@@ -558,6 +572,20 @@
     def _():
         for copy in last_copies():
             copy.wait_send()
+
+
+def write_out(grid_in, mesh_in, proc_in, weights_in, grid_out, mesh_out, proc_out, enc_out, dec_out, sem):
+    copies = [
+        pltpu.make_async_copy(grid_in, grid_out.at[0, 0], sem.at[0]),
+        pltpu.make_async_copy(mesh_in, mesh_out.at[0, 0], sem.at[1]),
+        pltpu.make_async_copy(proc_in, proc_out.at[0, 0], sem.at[2]),
+        pltpu.make_async_copy(weights_in.at[0], enc_out, sem.at[3]),
+        pltpu.make_async_copy(weights_in.at[1], dec_out, sem.at[4]),
+    ]
+    for copy in copies:
+        copy.start()
+    for copy in copies:
+        copy.wait()
 
 
 def shards(
@@ -574,17 +602,6 @@
     dec_send,
     dec_recv,
 ):
-    index = jnp.concatenate(
-        [
-            enc_send[0, 0],
-            enc_recv[0, 0],
-            jnp.broadcast_to(enc_live[0], (4, 128)),
-            dec_send[0, 0],
-            dec_recv[0, 0],
-            jnp.zeros((2, 128), I32),
-        ],
-        0,
-    )
     grad_scale = 1.0 / math.sqrt(4 * 64 * 128)
     vmem = pltpu.VMEM
     dma = pltpu.SemaphoreType.DMA
@@ -594,11 +611,10 @@
             jax.ShapeDtypeStruct((GRID, D), BF16),
             jax.ShapeDtypeStruct((NODES, D), BF16),
             jax.ShapeDtypeStruct((NODES, D), BF16),
-            jax.ShapeDtypeStruct((24, D), F32),
-            jax.ShapeDtypeStruct((24, D), F32),
+            jax.ShapeDtypeStruct((2, 3, 8, D), F32),
         ),
-        in_specs=[pl.BlockSpec(memory_space=pl.ANY)] * 8,
-        out_specs=(pl.BlockSpec(memory_space=pltpu.VMEM),) * 5,
+        in_specs=[pl.BlockSpec(memory_space=pltpu.HBM)] * 12,
+        out_specs=(pl.BlockSpec(memory_space=pltpu.VMEM),) * 4,
         scratch_shapes=[
             vmem((5, D, D), BF16),
             vmem((2 * GRID, D), BF16),
@@ -606,7 +622,10 @@
             vmem((EXT, D), BF16),
             vmem((EXT, D), BF16),
             vmem((NODES, D), BF16),
+            vmem((2, 2, 2, 128), I32),
+            vmem((2, 2, 3, 1, 128), I32),
             vmem((2, 8, 128), I32),
+            vmem((1, 1, 1), I32),
             vmem((2 * GRID, D), BF16),
             vmem((EXT, D), BF16),
             vmem((768, D), F32),
@@ -625,10 +644,10 @@
             vmem((3, 2, 3, 32, 256), BF16),
             vmem((4, 48, 256), BF16),
             vmem((7, 48, 256), BF16),
-            vmem((2, 24, D), F32),
+            vmem((2, 48, 256), BF16),
             dma((5,)),
-            dma,
             dma((2,)),
+            dma((5,)),
             dma((2,)),
             dma((2,)),
             dma((9,)),
@@ -640,7 +659,7 @@
             dma((7,)),
             dma((2,)),
             dma((18,)),
-            dma((4,)),
+            dma((6,)),
             dma((9,)),
             dma((18,)),
             dma((18,)),
@@ -652,23 +671,39 @@
         ),
         name="edge_layer",
     )(
-        grid_latent[0, 0],
-        grid_cot[0, 0],
-        mesh_latent[0, 0],
-        mesh_cot[0, 0],
-        processed[0, 0],
-        enc_weights,
-        dec_weights,
-        index,
+        *(
+            array if array is enc_live else pltpu.with_memory_space_constraint(array, pltpu.HBM)
+            for array in (
+                grid_latent[0, 0],
+                grid_cot[0, 0],
+                mesh_latent[0, 0],
+                mesh_cot[0, 0],
+                processed[0, 0],
+                enc_weights,
+                dec_weights,
+                enc_send[0, 0],
+                enc_recv[0, 0],
+                enc_live,
+                dec_send.reshape(3, 1, 128),
+                dec_recv.reshape(3, 1, 128),
+            )
+        )
     )
-    grid_grad, mesh_grad, proc_grad, enc_grads, dec_grads = outs
-    return (
-        grid_grad[None, None],
-        mesh_grad[None, None],
-        proc_grad[None, None],
-        enc_grads.reshape(3, 8, D),
-        dec_grads.reshape(3, 8, D),
-    )
+    return pl.pallas_call(
+        write_out,
+        out_shape=(
+            jax.ShapeDtypeStruct((1, 1, GRID, D), BF16),
+            jax.ShapeDtypeStruct((1, 1, NODES, D), BF16),
+            jax.ShapeDtypeStruct((1, 1, NODES, D), BF16),
+            jax.ShapeDtypeStruct((3, 8, D), F32),
+            jax.ShapeDtypeStruct((3, 8, D), F32),
+        ),
+        in_specs=[pl.BlockSpec(memory_space=pltpu.VMEM)] * 4,
+        out_specs=(pl.BlockSpec(memory_space=pltpu.HBM),) * 5,
+        scratch_shapes=[dma((5,))],
+        compiler_params=pltpu.CompilerParams(vmem_limit_bytes=2 * 2**20),
+        name="write_out",
+    )(*(pltpu.with_memory_space_constraint(array, pltpu.VMEM) for array in outs))
 
 
 def solution(mesh):

time: 67.3 us -> 51.2 us (0.76)
  local copies, waits for them, and re-layouts: 11.7 us -> 0 us
  Pallas kernels: 53.9 us -> 49.8 us
    unnamed x20 -> x0, local copies, waits for them, and re-layouts: 11 us -> none
    pallas_call x1, Pallas kernels: 53.9 us -> 49 us  [shards(): pl.pallas_call(lambda *refs: kernel(*refs, grad_scale), out_shape=(jax.Sh...]
    pallas_call x0 -> x1, Pallas kernels: none -> 0.77 us  [shards(): pl.pallas_call(write_out, out_shape=(jax.ShapeDtypeStruct((1, 1, GRID, D)...]
    concatenate x1 -> x0, local copies, waits for them, and re-layouts: 0.73 us -> none  [shards(): jnp.concatenate([enc_send[0, 0], enc_recv[0, 0], jnp.broadcast_to(enc_liv...]
where the time goes in v2:
time: 51.2 us; the launch traced here: 51.1 us
  Pallas kernels  49.8 us (97%)
  between operations  1.29 us (3%)
    pallas_call x1, Pallas kernels, shards(): pl.pallas_call(lambda *refs: kernel(*refs, grad_scale), out_shape=(jax.Sh...  49 us

profile of v2, /device:TPU:25, one launch (start us, length us, event | category | flops | bytes accessed | tf_op | source)
XLA Modules:
  0.0 51.1 jit_solution(9878304001287319540)
XLA Ops:
  1.3 49.0 %edge_layer.1 = (bf16[128,512]{1,0:T(8,128)(2,1)S(1)}, bf16[64,512]{1,0:T(8,128)(2,1)S(1)}, bf16[64,512]{1,0:T(8,128)(2,1)S(1)}, f32[2,3,8,512]{3,2,1,0:T(8,128)S(1)}) custom-call(bf16[128,512]{1,0:T(8,128)(2,1)} %bitcast.9, bf16[128,512]{1,0:T(8,128)(2,1)} %bitcast.10, bf16[64,512]{1,0:T(8,128)(2,1)} %bitcast.11, bf16[64,512]{1,0:T(8,128)(2,1)} %bitcast.12, ...), custom_call_target="tpu_custom_call" | custom-call | tf_op jit(solution)/shard_map/edge_layer/pallas_call | solution.py:608
  50.3 0.8 %write_out.1 = (bf16[1,1,128,512]{3,2,1,0:T(8,128)(2,1)}, bf16[1,1,64,512]{3,2,1,0:T(8,128)(2,1)}, bf16[1,1,64,512]{3,2,1,0:T(8,128)(2,1)}, f32[3,8,512]{2,1,0:T(8,128)}, f32[3,8,512]{2,1,0:T(8,128)}) custom-call(bf16[128,512]{1,0:T(8,128)(2,1)S(1)} %get-tuple-element.9.grid_in, bf16[64,512]{1,0:T(8,128)(2,1)S(1)} %get-tuple-element.10.mesh_in, ...), custom_call_target="tpu_custom_call" | custom-call | tf_op jit(solution)/shard_map/write_out/pallas_call | solution.py:692

commit v3 on v2

--- a/solution.py
+++ b/solution.py
@@ -90,6 +90,13 @@
     send3,
     recv3,
     final,
+    zsend,
+    zrecv,
+    xsend,
+    xrecv,
+    ysend,
+    yrecv,
+    last,
     w_sem,
     own_sem,
     i_sem,
@@ -110,6 +117,14 @@
     s2_sem,
     s3_sem,
     s4_sem,
+    zs_sem,
+    zr_sem,
+    xs_sem,
+    xr_sem,
+    ys_sem,
+    yr_sem,
+    ls_sem,
+    lr_sem,
     grad_scale,
 ):
     lat = lax.axis_index("lat")
@@ -194,34 +209,31 @@
         pl.semaphore_signal(barrier, inc=1, device_id=dev, device_id_type=MESH)
     pl.semaphore_wait(barrier, len(greeted))
 
-    def halo_copies(side, step):
+    def halo_copy(which, side, step):
         to_yh = yh if side == 0 else 1 - yh
         slot = (lat - to_yh) * 3 + 1 - step
         rows = pl.ds(pl.multiple_of(slot * NODES, NODES), NODES)
         at = side * 9 + (step + 1) * 3
         enc_dev = (to_yh * 2, sector(step))
         dec_dev = (to_yh * 2 + 1, sector(step))
-        return (
-            rcopy(mesh_ref, mext.at[rows], hs_sem.at[at], m_sem.at[slot], enc_dev),
-            rcopy(mcot_ref, text.at[rows], hs_sem.at[at + 1], t_sem.at[slot], enc_dev),
-            rcopy(proc_ref, mext.at[rows], hs_sem.at[at + 2], m_sem.at[slot], dec_dev),
-        )
+        if which == 0:
+            return rcopy(mesh_ref, mext.at[rows], hs_sem.at[at], m_sem.at[slot], enc_dev)
+        if which == 1:
+            return rcopy(mcot_ref, text.at[rows], hs_sem.at[at + 1], t_sem.at[slot], enc_dev)
+        return rcopy(proc_ref, mext.at[rows], hs_sem.at[at + 2], m_sem.at[slot], dec_dev)
 
     def each_halo(which, action):
         @pl.when(adjacent)
         def _():
             for step in (1, -1, 0):
-                for w in which:
-                    action(halo_copies(1, step)[w])
+                action(halo_copy(which, 1, step))
 
         for step in (1, -1):
-            for w in which:
-                action(halo_copies(0, step)[w])
-
-        @pl.when(core == (0 if 2 in which else 1))
+            action(halo_copy(which, 0, step))
+
+        @pl.when(core == (0 if which == 2 else 1))
         def _():
-            for w in which:
-                action(halo_copies(0, 0)[w])
+            action(halo_copy(which, 0, 0))
 
     cross_band = 2 - 2 * yh
 
@@ -240,11 +252,12 @@
             action(rcopy(erecv_ref, ebuf.at[1, 1], ss_sem.at[4], i_sem.at[3], sib))
             action(rcopy(lbuf.at[1], lbuf.at[1], ss_sem.at[5], i_sem.at[4], sib))
 
-    each_halo((2,), lambda copy: copy.start())
+    each_halo(2, lambda copy: copy.start())
+    each_halo(0, lambda copy: copy.start())
     arrived(lone, own_sem.at[1])
     lbuf[core] = jnp.broadcast_to(lone[0], (8, 128))
     each_swap(lambda copy: copy.start())
-    each_halo((0, 1), lambda copy: copy.start())
+    each_halo(1, lambda copy: copy.start())
 
     @pl.when(jnp.logical_not(adjacent))
     def _():
@@ -301,6 +314,36 @@
             for copy in stage1_copies(mat, half):
                 copy.start()
 
+    def z_copies():
+        copies = []
+        for step in (4, 3, 5, 2, 6, 1, 7):
+            to = lax.rem(z + step, 8)
+            copies.append(rcopy(zsend.at[to], zrecv.at[step - 1], zs_sem.at[step - 1], zr_sem.at[step - 1], z_dev(to)))
+        return copies
+
+    def x_copies():
+        copies = []
+        for step in (2, 1, 3):
+            to = lax.rem(x + step, 4)
+            copies.append(rcopy(xsend.at[to], xrecv.at[step - 1], xs_sem.at[step - 1], xr_sem.at[step - 1], x_dev(to)))
+        return copies
+
+    def y_copies():
+        copies = []
+        for step in (2, 1, 3):
+            to = lax.rem(y + step, 4)
+            copies.append(rcopy(ysend.at[lax.rem(to, 2)], yrecv.at[y], ys_sem.at[step - 1], yr_sem.at[y], y_dev(to)))
+        return copies
+
+    def sibling_copy():
+        return rcopy(last.at[core], last.at[core], ls_sem, lr_sem, sib)
+
+    def send_out_matrix():
+        for zz in range(8):
+            zsend[zz] = dwbuf[zz * 64 : (zz + 1) * 64].astype(BF16)
+        for copy in z_copies():
+            copy.start()
+
     def fold_copies(side, step):
         copies = []
         for which in ((0, 1) if side == 0 else (2,)):
@@ -313,21 +356,13 @@
             )
         return copies
 
-    def each_fold(action):
+    def each_fold(role, action):
         for step in (1, -1, 0):
             action(fold_copies(1, step)[0])
         for step in (1, -1):
             for copy in fold_copies(0, step):
                 action(copy)
-        to_first, to_second = fold_copies(0, 0)
-
-        @pl.when(core == 0)
-        def _():
-            action(to_second)
-
-        @pl.when(core == 1)
-        def _():
-            action(to_first)
+        action(fold_copies(0, 0)[1 - role])
 
     def gsum_copy():
         other = pl.ds(pl.multiple_of((1 - core) * GRID, GRID), GRID)
@@ -387,30 +422,32 @@
             wait_band(band)
             rows = pl.ds(pl.multiple_of(band * 192, 192), 192)
             mproj[rows] = dot(mext[rows], wts[w_mesh]).astype(BF16)
+        m_picks = []
+        for b in (0, 1):
+            rows = slice(b * edges, (b + 1) * edges)
+            m_picks.append(jnp.concatenate([pick_cols(r, EXT) for r in mesh_rows[b]], 0))
+            pre = dot(m_picks[b], mproj[...]) + gpart[rows]
+            gate = 1.0 / (1.0 + jnp.exp(-pre))
+            hid[rows] = (pre * gate).astype(BF16)
+            gpart[rows] = gate * (1.0 + pre * (1.0 - gate))
         if role == 0:
             for band in range(3):
                 wait_cot(band)
-        for b in (0, 1):
-            rows = slice(b * edges, (b + 1) * edges)
-            m_pick = jnp.concatenate([pick_cols(r, EXT) for r in mesh_rows[b]], 0)
-            pre = dot(m_pick, mproj[...]) + gpart[rows]
-            if role == 0:
+            for b in (0, 1):
+                rows = slice(b * edges, (b + 1) * edges)
                 place = lax.broadcasted_iota(I32, (edges, D), 0)
                 live = lbuf[b, 0:1, 0:1]
-                picked = jnp.where(place < live, dot(m_pick, text[...]), 0.0).astype(BF16)
+                picked = jnp.where(place < live, dot(m_picks[b], text[...]), 0.0).astype(BF16)
                 msg[rows] = picked
-                grown = dot_bt(picked, wts[4])
-            else:
-                grown = back[rows]
-            gate = 1.0 / (1.0 + jnp.exp(-pre))
-            hid[rows] = (pre * gate).astype(BF16)
-            pgrad[rows] = (grown * (gate * (1.0 + pre * (1.0 - gate)))).astype(BF16)
+                back[rows] = dot_bt(picked, wts[4])
         every = slice(0, 2 * edges)
         dwbuf[...] = dot_at(hid[every], msg[every])
-        send_matrix(2)
+        send_out_matrix()
+        pgrad[every] = (back[every] * gpart[every]).astype(BF16)
         m_turn = jnp.concatenate([pick_rows(r, EXT) for b in (0, 1) for r in mesh_rows[b]], 1)
         part[...] = dot(m_turn, pgrad[every]).astype(BF16)
         if role == 1:
+            each_fold(1, lambda copy: copy.start())
             dwbuf[...] = dot_at(mext[...], part[...])
             send_matrix(0)
         for b in (0, 1):
@@ -444,7 +481,7 @@
 
     arrived(town, own_sem.at[0])
 
-    for mat in (2, 0, 1):
+    for mat in (0, 1):
         for half in (0, 1):
             for step in range(3):
                 sem = (mat * 2 + half) * 3 + step
@@ -459,14 +496,30 @@
             for copy in stage2_copies(mat, half):
                 copy.start()
 
-    each_fold(lambda copy: copy.start())
-
-    gboth[core] = gsum[own_rows]
-    arrived(gboth.at[1 - core], gs_sem)
-    grid_out[...] = (call[own_rows].astype(F32) + dot_bt(gboth[0], wts[0]) + dot_bt(gboth[1], wts[3])).astype(BF16)
-
-    sums = []
-    for mat in range(3):
+    total = zsend[z].astype(F32)
+    for step in range(1, 8):
+        arrived(zrecv.at[step - 1], zr_sem.at[step - 1])
+        total = total + zrecv[step - 1].astype(F32)
+    for xx in range(4):
+        xsend[xx] = jnp.concatenate([total[xx * 8 : xx * 8 + 8], total[32 + xx * 8 : 40 + xx * 8]], 0).astype(BF16)
+    for copy in x_copies():
+        copy.start()
+
+    holds = lax.div(z, 4) == yh
+
+    def each_stage3(mat, action):
+        for step in (4, 3, 5, 2, 6, 1, 7):
+            to = lax.rem(z + step, 8)
+
+            @pl.when(lax.div(to, 4) == yh)
+            def _():
+                sem = mat * 7 + step - 1
+                action(
+                    rcopy(send3.at[mat, lax.rem(to, 4)], recv3.at[mat, step - 1], s3_sem.at[sem], r3_sem.at[sem], z_dev(to))
+                )
+
+    def stage3(mat):
+        sums = []
         for half in (0, 1):
             for step in range(3):
                 sem = (mat * 2 + half) * 3 + step
@@ -476,21 +529,57 @@
             for step in range(3):
                 total = total + recv2[mat, half, step].astype(F32)
             sums.append(total)
-    for q in range(4):
-        send3[q] = jnp.concatenate([s[q * 8 : (q + 1) * 8] for s in sums], 0).astype(BF16)
-
-    holds = lax.div(z, 4) == yh
-
-    def stage3_copy(step):
-        to = lax.rem(z + step, 8)
-        return (
-            lax.div(to, 4) == yh,
-            rcopy(send3.at[lax.rem(to, 4)], recv3.at[step - 1], s3_sem.at[step - 1], r3_sem.at[step - 1], z_dev(to)),
-        )
-
-    for step in (4, 3, 5, 2, 6, 1, 7):
-        goes, copy = stage3_copy(step)
-        pl.when(goes)(copy.start)
+        for q in range(4):
+            send3[mat, q] = jnp.concatenate([t[q * 8 : (q + 1) * 8] for t in sums], 0).astype(BF16)
+        each_stage3(mat, lambda copy: copy.start())
+
+    stage3(0)
+
+    @pl.when(core == 0)
+    def _():
+        each_fold(0, lambda copy: copy.start())
+
+    stage3(1)
+
+    total = xsend[x].astype(F32)
+    for step in range(1, 4):
+        arrived(xrecv.at[step - 1], xr_sem.at[step - 1])
+        total = total + xrecv[step - 1].astype(F32)
+    ysend[0] = total[0:8]
+    ysend[1] = total[8:16]
+    for copy in y_copies():
+        copy.start()
+
+    gboth[core] = gsum[own_rows]
+    arrived(gboth.at[1 - core], gs_sem)
+    grid_out[...] = (call[own_rows].astype(F32) + dot_bt(gboth[0], wts[0]) + dot_bt(gboth[1], wts[3])).astype(BF16)
+
+    def last_copies():
+        devs = (((1 - yh) * 2 + core, lon), ((1 - yh) * 2 + 1 - core, lon), sib)
+        return [rcopy(final.at[core], final.at[core], s4_sem.at[k], r4_sem.at[core], dev) for k, dev in enumerate(devs)]
+
+    @pl.when(holds)
+    def _():
+        totals = []
+        for mat in (0, 1):
+            for step in range(1, 8):
+                arrived(recv3.at[mat, step - 1], r3_sem.at[mat * 7 + step - 1])
+        for mat in (0, 1):
+            total = send3[mat, lax.rem(z, 4)].astype(F32)
+            for step in range(1, 8):
+                total = total + recv3[mat, step - 1].astype(F32)
+            totals.append(total)
+        total = jnp.concatenate(totals, 0)
+        final[core] = (total * grad_scale).astype(BF16)
+        for copy in last_copies():
+            copy.start()
+
+    yrecv[y] = ysend[yl]
+    for step in (1, 3, 2):
+        beyond = lax.rem(y + step, 4)
+        arrived(yrecv.at[beyond], yr_sem.at[beyond])
+    last[core] = (yrecv[0] + yrecv[1] + yrecv[2] + yrecv[3]) * grad_scale
+    sibling_copy().start()
 
     def part_of(slot):
         return pl.ds(pl.multiple_of(slot * NODES, NODES), NODES)
@@ -528,19 +617,8 @@
     mesh_out[...] = (town[...].astype(F32) + dot_bt(folded(0), wts[1])).astype(BF16)
     proc_out[...] = dot_bt(folded(1), wts[2]).astype(BF16)
 
-    def last_copies():
-        devs = (((1 - yh) * 2 + core, lon), ((1 - yh) * 2 + 1 - core, lon), sib)
-        return [rcopy(final.at[core], final.at[core], s4_sem.at[k], r4_sem.at[core], dev) for k, dev in enumerate(devs)]
-
     @pl.when(holds)
     def _():
-        total = send3[lax.rem(z, 4)].astype(F32)
-        for step in (1, 7, 2, 6, 3, 5, 4):
-            arrived(recv3.at[step - 1], r3_sem.at[step - 1])
-            total = total + recv3[step - 1].astype(F32)
-        final[core] = (total * grad_scale).astype(BF16)
-        for copy in last_copies():
-            copy.start()
         arrived(final.at[1 - core], r4_sem.at[1 - core])
 
     @pl.when(jnp.logical_not(holds))
@@ -548,25 +626,35 @@
         arrived(final.at[0], r4_sem.at[0])
         arrived(final.at[1], r4_sem.at[1])
 
+    arrived(last.at[1 - core], lr_sem)
     for role in (0, 1):
         pieces = final[role].astype(F32)
-        for mat in range(3):
+        weights_out[role, 2] = last[role]
+        for mat in (0, 1):
             weights_out[role, mat, :, 0:256] = pieces[mat * 16 : mat * 16 + 8]
             weights_out[role, mat, :, 256:512] = pieces[mat * 16 + 8 : mat * 16 + 16]
 
     each_swap(lambda copy: copy.wait_send())
-    each_halo((2,), lambda copy: copy.wait_send())
-    each_halo((0, 1), lambda copy: copy.wait_send())
-    each_fold(lambda copy: copy.wait_send())
+    for which in range(3):
+        each_halo(which, lambda copy: copy.wait_send())
+    @pl.when(core == 0)
+    def _():
+        each_fold(0, lambda copy: copy.wait_send())
+
+    @pl.when(core == 1)
+    def _():
+        each_fold(1, lambda copy: copy.wait_send())
+
 
     gsum_copy().wait_send()
-    for mat in range(3):
+    for copy in z_copies() + x_copies() + y_copies() + [sibling_copy()]:
+        copy.wait_send()
+    for mat in (0, 1):
         for half in (0, 1):
             for copy in stage1_copies(mat, half) + stage2_copies(mat, half):
                 copy.wait_send()
-    for step in range(1, 8):
-        goes, copy = stage3_copy(step)
-        pl.when(goes)(copy.wait_send)
+    for mat in (0, 1):
+        each_stage3(mat, lambda copy: copy.wait_send())
 
     @pl.when(holds)
     def _():
@@ -638,13 +726,20 @@
             vmem((2, GRID, D), BF16),
             vmem((2, 6, NODES, D), BF16),
             vmem((D, D), F32),
-            vmem((3, 2, 4, 128, 256), BF16),
-            vmem((3, 2, 3, 128, 256), BF16),
-            vmem((3, 2, 4, 32, 256), BF16),
-            vmem((3, 2, 3, 32, 256), BF16),
-            vmem((4, 48, 256), BF16),
-            vmem((7, 48, 256), BF16),
-            vmem((2, 48, 256), BF16),
+            vmem((2, 2, 4, 128, 256), BF16),
+            vmem((2, 2, 3, 128, 256), BF16),
+            vmem((2, 2, 4, 32, 256), BF16),
+            vmem((2, 2, 3, 32, 256), BF16),
+            vmem((2, 4, 16, 256), BF16),
+            vmem((2, 7, 16, 256), BF16),
+            vmem((2, 32, 256), BF16),
+            vmem((8, 64, D), BF16),
+            vmem((7, 64, D), BF16),
+            vmem((4, 16, D), BF16),
+            vmem((3, 16, D), BF16),
+            vmem((2, 8, D), F32),
+            vmem((4, 8, D), F32),
+            vmem((2, 8, D), F32),
             dma((5,)),
             dma((2,)),
             dma((5,)),
@@ -656,15 +751,23 @@
             dma,
             dma((18,)),
             dma((18,)),
-            dma((7,)),
+            dma((21,)),
             dma((2,)),
             dma((18,)),
             dma((6,)),
             dma((9,)),
             dma((18,)),
             dma((18,)),
+            dma((21,)),
+            dma((3,)),
+            dma((7,)),
             dma((7,)),
             dma((3,)),
+            dma((3,)),
+            dma((3,)),
+            dma((4,)),
+            dma,
+            dma,
         ],
         compiler_params=pltpu.CompilerParams(
             collective_id=0, has_side_effects=True, vmem_limit_bytes=48 * 2**20

time: 51.2 us -> 49.8 us (0.973)
  the two profiles are of different devices: /device:TPU:25 before, /device:TPU:1 now
where the time goes in v3:
time: 49.8 us; the launch traced here: 49.7 us
  Pallas kernels  48.4 us (97%)
  between operations  1.29 us (3%)
    pallas_call x1, Pallas kernels, shards(): pl.pallas_call(lambda *refs: kernel(*refs, grad_scale), out_shape=(jax.Sh...  47.6 us

profile of v3, /device:TPU:1, one launch (start us, length us, event | category | flops | bytes accessed | tf_op | source)
XLA Modules:
  0.0 49.7 jit_solution(1158001540253972011)
XLA Ops:
  1.3 47.6 %edge_layer.1 = (bf16[128,512]{1,0:T(8,128)(2,1)S(1)}, bf16[64,512]{1,0:T(8,128)(2,1)S(1)}, bf16[64,512]{1,0:T(8,128)(2,1)S(1)}, f32[2,3,8,512]{3,2,1,0:T(8,128)S(1)}) custom-call(bf16[128,512]{1,0:T(8,128)(2,1)} %bitcast.9, bf16[128,512]{1,0:T(8,128)(2,1)} %bitcast.10, bf16[64,512]{1,0:T(8,128)(2,1)} %bitcast.11, bf16[64,512]{1,0:T(8,128)(2,1)} %bitcast.12, ...), custom_call_target="tpu_custom_call" | custom-call | tf_op jit(solution)/shard_map/edge_layer/pallas_call | solution.py:696
  48.9 0.8 %write_out.1 = (bf16[1,1,128,512]{3,2,1,0:T(8,128)(2,1)}, bf16[1,1,64,512]{3,2,1,0:T(8,128)(2,1)}, bf16[1,1,64,512]{3,2,1,0:T(8,128)(2,1)}, f32[3,8,512]{2,1,0:T(8,128)}, f32[3,8,512]{2,1,0:T(8,128)}) custom-call(bf16[128,512]{1,0:T(8,128)(2,1)S(1)} %get-tuple-element.9.grid_in, bf16[64,512]{1,0:T(8,128)(2,1)S(1)} %get-tuple-element.10.mesh_in, ...), custom_call_target="tpu_custom_call" | custom-call | tf_op jit(solution)/shard_map/write_out/pallas_call | solution.py:795

commit v4 on v3

--- a/solution.py
+++ b/solution.py
@@ -71,6 +71,9 @@
     dbuf,
     lbuf,
     lone,
+    mpick,
+    mturn,
+    gturn,
     gproj,
     mproj,
     gpart,
@@ -265,15 +268,32 @@
             for k in (3, 4, 5):
                 fold[role, k] = jnp.zeros((NODES, D), BF16)
 
+    def by_core(of_core0, of_core1):
+        if isinstance(of_core0, tuple):
+            return tuple(jnp.where(core == 0, a, b) for a, b in zip(of_core0, of_core1))
+        return jnp.where(core == 0, of_core0, of_core1)
+
+    def toward_x(step):
+        to = lax.rem(x + step, 4)
+        return to, x_dev(to)
+
+    def toward_y(step):
+        to = lax.rem(y + step, 4)
+        return to, y_dev(to)
+
+    def toward(mat, half, stage, step):
+        if mat == 2:
+            of_x, of_y = toward_x(step), toward_y(step)
+            first, second = (of_y, of_x) if stage == 1 else (of_x, of_y)
+            return by_core(first[0], second[0]), by_core(first[1], second[1])
+        return toward_x(step) if half + 1 == stage else toward_y(step)
+
+    units = ((0, 0), (0, 1), (1, 0), (1, 1), (2, 0))
+
     def stage1_copies(mat, half):
         copies = []
         for step in (1, 3, 2):
-            if half == 0:
-                to = lax.rem(x + step, 4)
-                dev = x_dev(to)
-            else:
-                to = lax.rem(y + step, 4)
-                dev = y_dev(to)
+            to, dev = toward(mat, half, 1, step)
             sem = (mat * 2 + half) * 3 + step - 1
             copies.append(
                 rcopy(send1.at[mat, half, to], recv1.at[mat, half, step - 1], s1_sem.at[sem], r1_sem.at[sem], dev)
@@ -283,31 +303,29 @@
     def stage2_copies(mat, half):
         copies = []
         for step in (1, 3, 2):
-            if half == 0:
-                to = lax.rem(y + step, 4)
-                dev = y_dev(to)
-            else:
-                to = lax.rem(x + step, 4)
-                dev = x_dev(to)
+            to, dev = toward(mat, half, 2, step)
             sem = (mat * 2 + half) * 3 + step - 1
             copies.append(
                 rcopy(send2.at[mat, half, to], recv2.at[mat, half, step - 1], s2_sem.at[sem], r2_sem.at[sem], dev)
             )
         return copies
 
+    def row_group(xx, yy, zz):
+        return ((yy // 2) * 4 + zz) * 64 + (yy % 2) * 32 + xx * 8
+
     def send_matrix(mat):
         for xx in range(4):
             pieces = []
             for yy in range(4):
                 for zz in range(4):
-                    row = ((yy // 2) * 4 + zz) * 64 + (yy % 2) * 32 + xx * 8
+                    row = row_group(xx, yy, zz)
                     pieces.append(dwbuf[row : row + 8, 0:256])
             send1[mat, 0, xx] = jnp.concatenate(pieces, 0).astype(BF16)
         for yy in range(4):
             pieces = []
             for xx in range(4):
                 for zz in range(4):
-                    row = ((yy // 2) * 4 + zz) * 64 + (yy % 2) * 32 + xx * 8
+                    row = row_group(xx, yy, zz)
                     pieces.append(dwbuf[row : row + 8, 256:512])
             send1[mat, 1, yy] = jnp.concatenate(pieces, 0).astype(BF16)
         for half in (0, 1):
@@ -338,10 +356,19 @@
     def sibling_copy():
         return rcopy(last.at[core], last.at[core], ls_sem, lr_sem, sib)
 
-    def send_out_matrix():
+    def send_out_matrix(role):
         for zz in range(8):
-            zsend[zz] = dwbuf[zz * 64 : (zz + 1) * 64].astype(BF16)
+            zsend[zz] = dwbuf[zz * 64 : (zz + 1) * 64, 0:256].astype(BF16)
         for copy in z_copies():
+            copy.start()
+        for to in range(4):
+            pieces = []
+            for other in range(4):
+                for zz in range(4):
+                    row = row_group(other, to, zz) if role == 0 else row_group(to, other, zz)
+                    pieces.append(dwbuf[row : row + 8, 256:512])
+            send1[2, 0, to] = jnp.concatenate(pieces, 0).astype(BF16)
+        for copy in stage1_copies(2, 0):
             copy.start()
 
     def fold_copies(side, step):
@@ -416,17 +443,21 @@
                 picked = dot(g_pick, call[b * GRID : (b + 1) * GRID]).astype(BF16)
                 msg[rows] = picked
                 back[rows] = dot_bt(picked, wts[4])
+        for b in (0, 1):
+            for q in range(blocks):
+                at = b * edges + q * 128
+                mpick[at : at + 128] = pick_cols(mesh_rows[b][q], EXT)
+                mturn[:, at : at + 128] = pick_rows(mesh_rows[b][q], EXT)
+                gturn[:, at : at + 128] = pick_rows(grid_rows[b][q], GRID)
         weight(w_mesh)
         for k in (0, 1, 2):
             band = (yh + k if k < 2 else cross_band)
             wait_band(band)
             rows = pl.ds(pl.multiple_of(band * 192, 192), 192)
             mproj[rows] = dot(mext[rows], wts[w_mesh]).astype(BF16)
-        m_picks = []
         for b in (0, 1):
             rows = slice(b * edges, (b + 1) * edges)
-            m_picks.append(jnp.concatenate([pick_cols(r, EXT) for r in mesh_rows[b]], 0))
-            pre = dot(m_picks[b], mproj[...]) + gpart[rows]
+            pre = dot(mpick[rows], mproj[...]) + gpart[rows]
             gate = 1.0 / (1.0 + jnp.exp(-pre))
             hid[rows] = (pre * gate).astype(BF16)
             gpart[rows] = gate * (1.0 + pre * (1.0 - gate))
@@ -437,22 +468,22 @@
                 rows = slice(b * edges, (b + 1) * edges)
                 place = lax.broadcasted_iota(I32, (edges, D), 0)
                 live = lbuf[b, 0:1, 0:1]
-                picked = jnp.where(place < live, dot(m_picks[b], text[...]), 0.0).astype(BF16)
+                picked = jnp.where(place < live, dot(mpick[rows], text[...]), 0.0).astype(BF16)
                 msg[rows] = picked
-                back[rows] = dot_bt(picked, wts[4])
         every = slice(0, 2 * edges)
         dwbuf[...] = dot_at(hid[every], msg[every])
-        send_out_matrix()
+        send_out_matrix(role)
+        if role == 0:
+            back[every] = dot_bt(msg[every], wts[4])
         pgrad[every] = (back[every] * gpart[every]).astype(BF16)
-        m_turn = jnp.concatenate([pick_rows(r, EXT) for b in (0, 1) for r in mesh_rows[b]], 1)
-        part[...] = dot(m_turn, pgrad[every]).astype(BF16)
+        part[...] = dot(mturn[:, every], pgrad[every]).astype(BF16)
         if role == 1:
             each_fold(1, lambda copy: copy.start())
             dwbuf[...] = dot_at(mext[...], part[...])
             send_matrix(0)
         for b in (0, 1):
-            g_turn = jnp.concatenate([pick_rows(r, GRID) for r in grid_rows[b]], 1)
-            gsum[b * GRID : (b + 1) * GRID] = dot(g_turn, pgrad[b * edges : (b + 1) * edges]).astype(BF16)
+            rows = slice(b * edges, (b + 1) * edges)
+            gsum[b * GRID : (b + 1) * GRID] = dot(gturn[:, rows], pgrad[rows]).astype(BF16)
         gsum_copy().start()
         dwbuf[...] = dot_at(gall[...], gsum[...])
         send_matrix(0 if role == 0 else 1)
@@ -481,20 +512,19 @@
 
     arrived(town, own_sem.at[0])
 
-    for mat in (0, 1):
-        for half in (0, 1):
-            for step in range(3):
-                sem = (mat * 2 + half) * 3 + step
-                arrived(recv1.at[mat, half, step], r1_sem.at[sem])
-            own = x if half == 0 else y
-            total = send1[mat, half, own].astype(F32)
-            for step in range(3):
-                total = total + recv1[mat, half, step].astype(F32)
-            total = total.astype(BF16)
-            for k in range(4):
-                send2[mat, half, k] = total[k * 32 : (k + 1) * 32]
-            for copy in stage2_copies(mat, half):
-                copy.start()
+    for mat, half in ((2, 0), (0, 0), (0, 1), (1, 0), (1, 1)):
+        for step in range(3):
+            sem = (mat * 2 + half) * 3 + step
+            arrived(recv1.at[mat, half, step], r1_sem.at[sem])
+        own = by_core(y, x) if mat == 2 else (x, y)[half]
+        total = send1[mat, half, own].astype(F32)
+        for step in range(3):
+            total = total + recv1[mat, half, step].astype(F32)
+        total = total.astype(BF16)
+        for k in range(4):
+            send2[mat, half, k] = total[k * 32 : (k + 1) * 32]
+        for copy in stage2_copies(mat, half):
+            copy.start()
 
     total = zsend[z].astype(F32)
     for step in range(1, 8):
@@ -520,19 +550,23 @@
 
     def stage3(mat):
         sums = []
-        for half in (0, 1):
+        for half in (0, 1) if mat < 2 else (0,):
             for step in range(3):
                 sem = (mat * 2 + half) * 3 + step
                 arrived(recv2.at[mat, half, step], r2_sem.at[sem])
-            own = y if half == 0 else x
+            own = by_core(x, y) if mat == 2 else (y, x)[half]
             total = send2[mat, half, own].astype(F32)
             for step in range(3):
                 total = total + recv2[mat, half, step].astype(F32)
             sums.append(total)
         for q in range(4):
-            send3[mat, q] = jnp.concatenate([t[q * 8 : (q + 1) * 8] for t in sums], 0).astype(BF16)
+            pieces = [t[q * 8 : (q + 1) * 8] for t in sums]
+            if mat == 2:
+                pieces.append(jnp.zeros((8, 256), F32))
+            send3[mat, q] = jnp.concatenate(pieces, 0).astype(BF16)
         each_stage3(mat, lambda copy: copy.start())
 
+    stage3(2)
     stage3(0)
 
     @pl.when(core == 0)
@@ -554,6 +588,16 @@
     arrived(gboth.at[1 - core], gs_sem)
     grid_out[...] = (call[own_rows].astype(F32) + dot_bt(gboth[0], wts[0]) + dot_bt(gboth[1], wts[3])).astype(BF16)
 
+    each_swap(lambda copy: copy.wait_send())
+    for which in range(3):
+        each_halo(which, lambda copy: copy.wait_send())
+    gsum_copy().wait_send()
+    for copy in z_copies() + x_copies():
+        copy.wait_send()
+    for mat, half in units:
+        for copy in stage1_copies(mat, half) + stage2_copies(mat, half):
+            copy.wait_send()
+
     def last_copies():
         devs = (((1 - yh) * 2 + core, lon), ((1 - yh) * 2 + 1 - core, lon), sib)
         return [rcopy(final.at[core], final.at[core], s4_sem.at[k], r4_sem.at[core], dev) for k, dev in enumerate(devs)]
@@ -561,10 +605,10 @@
     @pl.when(holds)
     def _():
         totals = []
-        for mat in (0, 1):
+        for mat in (2, 0, 1):
             for step in range(1, 8):
                 arrived(recv3.at[mat, step - 1], r3_sem.at[mat * 7 + step - 1])
-        for mat in (0, 1):
+        for mat in range(3):
             total = send3[mat, lax.rem(z, 4)].astype(F32)
             for step in range(1, 8):
                 total = total + recv3[mat, step - 1].astype(F32)
@@ -629,14 +673,12 @@
     arrived(last.at[1 - core], lr_sem)
     for role in (0, 1):
         pieces = final[role].astype(F32)
-        weights_out[role, 2] = last[role]
+        weights_out[role, 2, :, 0:256] = last[role]
+        weights_out[role, 2, :, 256:512] = pieces[32:40]
         for mat in (0, 1):
             weights_out[role, mat, :, 0:256] = pieces[mat * 16 : mat * 16 + 8]
             weights_out[role, mat, :, 256:512] = pieces[mat * 16 + 8 : mat * 16 + 16]
 
-    each_swap(lambda copy: copy.wait_send())
-    for which in range(3):
-        each_halo(which, lambda copy: copy.wait_send())
     @pl.when(core == 0)
     def _():
         each_fold(0, lambda copy: copy.wait_send())
@@ -646,14 +688,9 @@
         each_fold(1, lambda copy: copy.wait_send())
 
 
-    gsum_copy().wait_send()
-    for copy in z_copies() + x_copies() + y_copies() + [sibling_copy()]:
+    for copy in y_copies() + [sibling_copy()]:
         copy.wait_send()
-    for mat in (0, 1):
-        for half in (0, 1):
-            for copy in stage1_copies(mat, half) + stage2_copies(mat, half):
-                copy.wait_send()
-    for mat in (0, 1):
+    for mat in range(3):
         each_stage3(mat, lambda copy: copy.wait_send())
 
     @pl.when(holds)
@@ -714,6 +751,9 @@
             vmem((2, 2, 3, 1, 128), I32),
             vmem((2, 8, 128), I32),
             vmem((1, 1, 1), I32),
+            vmem((768, EXT), BF16),
+            vmem((EXT, 768), BF16),
+            vmem((GRID, 768), BF16),
             vmem((2 * GRID, D), BF16),
             vmem((EXT, D), BF16),
             vmem((768, D), F32),
@@ -726,20 +766,20 @@
             vmem((2, GRID, D), BF16),
             vmem((2, 6, NODES, D), BF16),
             vmem((D, D), F32),
-            vmem((2, 2, 4, 128, 256), BF16),
-            vmem((2, 2, 3, 128, 256), BF16),
-            vmem((2, 2, 4, 32, 256), BF16),
-            vmem((2, 2, 3, 32, 256), BF16),
-            vmem((2, 4, 16, 256), BF16),
-            vmem((2, 7, 16, 256), BF16),
-            vmem((2, 32, 256), BF16),
-            vmem((8, 64, D), BF16),
-            vmem((7, 64, D), BF16),
-            vmem((4, 16, D), BF16),
-            vmem((3, 16, D), BF16),
-            vmem((2, 8, D), F32),
-            vmem((4, 8, D), F32),
-            vmem((2, 8, D), F32),
+            vmem((3, 2, 4, 128, 256), BF16),
+            vmem((3, 2, 3, 128, 256), BF16),
+            vmem((3, 2, 4, 32, 256), BF16),
+            vmem((3, 2, 3, 32, 256), BF16),
+            vmem((3, 4, 16, 256), BF16),
+            vmem((3, 7, 16, 256), BF16),
+            vmem((2, 48, 256), BF16),
+            vmem((8, 64, 256), BF16),
+            vmem((7, 64, 256), BF16),
+            vmem((4, 16, 256), BF16),
+            vmem((3, 16, 256), BF16),
+            vmem((2, 8, 256), F32),
+            vmem((4, 8, 256), F32),
+            vmem((2, 8, 256), F32),
             dma((5,)),
             dma((2,)),
             dma((5,)),

time: 49.8 us -> 49.4 us (level)
  the two profiles are of different devices: /device:TPU:1 before, /device:TPU:25 now
where the time goes in v4:
time: 49.4 us; the launch traced here: 48.5 us
  Pallas kernels  47.2 us (96%)
  between operations  1.29 us (3%)
    pallas_call x1, Pallas kernels, shards(): pl.pallas_call(lambda *refs: kernel(*refs, grad_scale), out_shape=(jax.Sh...  46.4 us

profile of v4, /device:TPU:25, one launch (start us, length us, event | category | flops | bytes accessed | tf_op | source)
XLA Modules:
  0.0 48.5 jit_solution(795316612826276686)
XLA Ops:
  1.3 46.4 %edge_layer.1 = (bf16[128,512]{1,0:T(8,128)(2,1)S(1)}, bf16[64,512]{1,0:T(8,128)(2,1)S(1)}, bf16[64,512]{1,0:T(8,128)(2,1)S(1)}, f32[2,3,8,512]{3,2,1,0:T(8,128)S(1)}) custom-call(bf16[128,512]{1,0:T(8,128)(2,1)} %bitcast.9, bf16[128,512]{1,0:T(8,128)(2,1)} %bitcast.10, bf16[64,512]{1,0:T(8,128)(2,1)} %bitcast.11, bf16[64,512]{1,0:T(8,128)(2,1)} %bitcast.12, ...), custom_call_target="tpu_custom_call" | custom-call | tf_op jit(solution)/shard_map/edge_layer/pallas_call | solution.py:733
  47.7 0.8 %write_out.1 = (bf16[1,1,128,512]{3,2,1,0:T(8,128)(2,1)}, bf16[1,1,64,512]{3,2,1,0:T(8,128)(2,1)}, bf16[1,1,64,512]{3,2,1,0:T(8,128)(2,1)}, f32[3,8,512]{2,1,0:T(8,128)}, f32[3,8,512]{2,1,0:T(8,128)}) custom-call(bf16[128,512]{1,0:T(8,128)(2,1)S(1)} %get-tuple-element.9.grid_in, bf16[64,512]{1,0:T(8,128)(2,1)S(1)} %get-tuple-element.10.mesh_in, ...), custom_call_target="tpu_custom_call" | custom-call | tf_op jit(solution)/shard_map/write_out/pallas_call | solution.py:835
